TPU v7x, 128 devices: a whole 4x4x4 slice. The times are simulated.
128 devices in a mesh: tm: 8 (over x_lo, z), space: 16 (over x_hi, y, core).
Axes of the slice: x: 4 (x_hi: 2, x_lo: 2; x = x_hi * 2 + x_lo), y: 4, z: 4, core: 2. Of those that a mesh axis runs over, the one named last changes fastest.
Arguments:
- query: bfloat16 [8, 1024, 4096], P('tm', 'space'), may hold values from -80 to 80
- key: bfloat16 [8, 1024, 4096], P('tm', 'space'), may hold values from -4 to 4
- value: bfloat16 [8, 1024, 4096], P('tm', 'space'), may hold values from -6 to 6
- widths: int32 [4, 8], replicated, may hold values from 0 to 7, as said below
Outputs:
- attended: bfloat16 [8, 1024, 4096], P('tm', 'space')
Inputs may be any that keep to these rules, and one draw needn't show every extreme that they name: `widths`: some entry is 0 and another is 7.
All inputs are finite; a program needn't handle non-finite values.
Results may differ from a plain program's by a relative error of at most 0.0049.
Values may be sent and summed in bfloat16 or wider, within the bound.
No kernel may reach another device: no remote copies, remote signals or barrier semaphores. Data moves between devices by JAX's collectives and lax.ppermute only.
A program may use at most 192 MiB of HBM per device.

v0:
```python
import jax
import jax.numpy as jnp
from jax import lax
from jax.sharding import PartitionSpec as P

HEADS = 32
HEAD_DIM = 128
BLK = 128


def shifted(value, axis, steps):
    count = lax.axis_size(axis)
    first, last = (max(0, -steps), min(count, count - steps))
    return lax.ppermute(value, axis, [(source, source + steps) for source in range(first, last)])


def on_device(query, key, value, widths):
    frame_index = lax.axis_index("tm")
    frame_count = lax.axis_size("tm")
    band_rows = query.shape[1]
    query_band = query.reshape(band_rows, HEADS, HEAD_DIM)
    key_band = key.reshape(band_rows, HEADS, HEAD_DIM)
    value_band = value.reshape(band_rows, HEADS, HEAD_DIM)
    local_query, local_key, local_value = (
        lax.all_to_all(query_band, "space", split_axis=1, concat_axis=0, tiled=True),
        lax.all_to_all(key_band, "space", split_axis=1, concat_axis=0, tiled=True),
        lax.all_to_all(value_band, "space", split_axis=1, concat_axis=0, tiled=True),
    )
    frame_tok = local_query.shape[0]
    local_heads = local_query.shape[1]
    frame_blocks = frame_tok // BLK
    levels = widths.shape[0]
    key_parts = [local_key]
    value_parts = [local_value]
    distance_parts = [jnp.zeros((frame_tok,), dtype=jnp.int32)]
    present_parts = [jnp.ones((frame_tok,), dtype=bool)]
    for distance in range(1, frame_count):
        for direction in (1, -1):
            shift_by = direction * distance
            source_frame = frame_index - shift_by
            moved_key_band, moved_value_band = shifted((key_band, value_band), "tm", shift_by)
            moved_key, moved_value = (
                lax.all_to_all(moved_key_band, "space", split_axis=1, concat_axis=0, tiled=True),
                lax.all_to_all(moved_value_band, "space", split_axis=1, concat_axis=0, tiled=True),
            )
            key_parts.append(moved_key)
            value_parts.append(moved_value)
            distance_parts.append(jnp.full((frame_tok,), distance, dtype=jnp.int32))
            present_parts.append(
                jnp.full((frame_tok,), (source_frame >= 0) & (source_frame < frame_count))
            )
    all_keys = jnp.transpose(jnp.concatenate(key_parts, 0), (1, 0, 2))
    all_values = jnp.transpose(jnp.concatenate(value_parts, 0), (1, 0, 2))
    key_distance = jnp.concatenate(distance_parts, 0)
    key_present = jnp.concatenate(present_parts, 0)
    key_count = key_distance.shape[0]
    key_block = jnp.tile(jnp.arange(frame_tok, dtype=jnp.int32) // BLK, key_count // frame_tok)
    key_level = jnp.zeros_like(key_distance)
    for level_index in range(levels):
        key_level = key_level + (key_distance > 1 << level_index).astype(jnp.int32)
    level_ids = jnp.arange(levels, dtype=jnp.int32)
    level_onehot = (key_level[:, None] == level_ids[None, :]).astype(jnp.float32)
    self_frame = key_distance == 0
    block_ids = jnp.arange(frame_blocks, dtype=jnp.int32)
    head_query = jnp.transpose(local_query, (1, 0, 2))
    block_rows = min(512, frame_tok)
    block_count = frame_tok // block_rows

    def one_block(begin_row):
        row_blocks = (begin_row + jnp.arange(block_rows, dtype=jnp.int32)) // BLK
        row_pick = (row_blocks[:, None] == block_ids[None, :]).astype(jnp.float32)
        row_widths = jnp.dot(
            row_pick, jnp.transpose(widths).astype(jnp.float32), precision=lax.Precision.HIGHEST
        )
        pair_width = jnp.dot(row_widths, level_onehot.T, precision=lax.Precision.HIGHEST)
        key_limit = jnp.where(self_frame[None, :], float(frame_blocks), pair_width)
        spread = jnp.abs(row_blocks[:, None] - key_block[None, :]).astype(jnp.float32)
        allowed = key_present[None, :] & (spread <= key_limit + 0.5)

        def one_head(operands):
            q_head, k_head, v_head = operands
            query_rows = lax.dynamic_slice_in_dim(q_head, begin_row, block_rows, 0)
            scores = jnp.dot(
                query_rows, k_head.T, preferred_element_type=jnp.float32
            ) * HEAD_DIM ** (-0.5)
            scores = jnp.where(allowed, scores, -jnp.inf)
            row_top = jnp.max(scores, axis=1, keepdims=True)
            exp_scores = jnp.exp(scores - row_top)
            weights = (exp_scores / jnp.sum(exp_scores, axis=1, keepdims=True)).astype(jnp.bfloat16)
            return jnp.dot(weights, v_head, preferred_element_type=jnp.float32).astype(jnp.bfloat16)

        return lax.map(one_head, (head_query, all_keys, all_values))

    result = lax.map(one_block, jnp.arange(block_count, dtype=jnp.int32) * block_rows)
    result = jnp.transpose(result, (0, 2, 1, 3)).reshape(frame_tok, local_heads, HEAD_DIM)
    returned = lax.all_to_all(result, "space", split_axis=0, concat_axis=1, tiled=True)
    return returned.reshape(1, band_rows, HEADS * HEAD_DIM)


def solution(mesh):
    return jax.shard_map(
        on_device,
        mesh=mesh,
        in_specs=(P("tm", "space", None), P("tm", "space", None), P("tm", "space", None), P()),
        out_specs=P("tm", "space", None),
        check_vma=False,
    )
```

profile of v0, /device:TPU:98, one launch (start us, length us, event | category | flops | bytes accessed | tf_op | source)
XLA Modules:
  0.0 880.4 jit_solution(6188937346606884441)
XLA Ops:
  12.3 10.2 %all-to-all-done.16 = bf16[64,32,128]{2,0,1:T(8,128)(2,1)S(1)} async-done(((bf16[64,32,128]{2,0,1:T(8,128)(2,1)}), bf16[64,32,128]{2,0,1:T(8,128)(2,1)S(1)}, u32[]{:S(2)}, u32[]{:S(2)}) %all-to-all-start.16) | async-done | bytes 524320 | tf_op jit(solution)/shard_map/all_to_all | solution.py:27
  60.2 10.0 %all-to-all-done.17 = bf16[64,32,128]{2,0,1:T(8,128)(2,1)S(1)} async-done(((bf16[64,32,128]{2,0,1:T(8,128)(2,1)}), bf16[64,32,128]{2,0,1:T(8,128)(2,1)S(1)}, u32[]{:S(2)}, u32[]{:S(2)}) %all-to-all-start.17) | async-done | bytes 524320 | tf_op jit(solution)/shard_map/all_to_all | solution.py:44
  93.8 9.0 %all-to-all-done.19 = bf16[64,32,128]{2,0,1:T(8,128)(2,1)} async-done(((bf16[64,32,128]{2,0,1:T(8,128)(2,1)}), bf16[64,32,128]{2,0,1:T(8,128)(2,1)}, u32[]{:S(2)}, u32[]{:S(2)}) %all-to-all-start.19) | async-done | bytes 524320 | tf_op jit(solution)/shard_map/all_to_all | solution.py:44
  127.0 9.0 %all-to-all-done.21 = bf16[64,32,128]{2,0,1:T(8,128)(2,1)} async-done(((bf16[64,32,128]{2,0,1:T(8,128)(2,1)}), bf16[64,32,128]{2,0,1:T(8,128)(2,1)}, u32[]{:S(2)}, u32[]{:S(2)}) %all-to-all-start.21) | async-done | bytes 524320 | tf_op jit(solution)/shard_map/all_to_all | solution.py:44
  160.6 9.0 %all-to-all-done.23 = bf16[64,32,128]{2,0,1:T(8,128)(2,1)} async-done(((bf16[64,32,128]{2,0,1:T(8,128)(2,1)}), bf16[64,32,128]{2,0,1:T(8,128)(2,1)}, u32[]{:S(2)}, u32[]{:S(2)}) %all-to-all-start.23) | async-done | bytes 524320 | tf_op jit(solution)/shard_map/all_to_all | solution.py:44
  194.4 9.0 %all-to-all-done.25 = bf16[64,32,128]{2,0,1:T(8,128)(2,1)} async-done(((bf16[64,32,128]{2,0,1:T(8,128)(2,1)}), bf16[64,32,128]{2,0,1:T(8,128)(2,1)}, u32[]{:S(2)}, u32[]{:S(2)}) %all-to-all-start.25) | async-done | bytes 524320 | tf_op jit(solution)/shard_map/all_to_all | solution.py:44
  228.1 9.0 %all-to-all-done.27 = bf16[64,32,128]{2,0,1:T(8,128)(2,1)} async-done(((bf16[64,32,128]{2,0,1:T(8,128)(2,1)}), bf16[64,32,128]{2,0,1:T(8,128)(2,1)}, u32[]{:S(2)}, u32[]{:S(2)}) %all-to-all-start.27) | async-done | bytes 524320 | tf_op jit(solution)/shard_map/all_to_all | solution.py:44
  261.8 9.0 %all-to-all-done.29 = bf16[64,32,128]{2,0,1:T(8,128)(2,1)} async-done(((bf16[64,32,128]{2,0,1:T(8,128)(2,1)}), bf16[64,32,128]{2,0,1:T(8,128)(2,1)}, u32[]{:S(2)}, u32[]{:S(2)}) %all-to-all-start.29) | async-done | bytes 524320 | tf_op jit(solution)/shard_map/all_to_all | solution.py:44
  295.1 9.0 %all-to-all-done.2 = bf16[64,32,128]{2,0,1:T(8,128)(2,1)} async-done(((bf16[64,32,128]{2,0,1:T(8,128)(2,1)}), bf16[64,32,128]{2,0,1:T(8,128)(2,1)}, u32[]{:S(2)}, u32[]{:S(2)}) %all-to-all-start.2) | async-done | bytes 524320 | tf_op jit(solution)/shard_map/all_to_all | solution.py:43
  395.5 9.0 %all-to-all-done.8 = bf16[64,32,128]{2,0,1:T(8,128)(2,1)} async-done(((bf16[64,32,128]{2,0,1:T(8,128)(2,1)}), bf16[64,32,128]{2,0,1:T(8,128)(2,1)}, u32[]{:S(2)}, u32[]{:S(2)}) %all-to-all-start.8) | async-done | bytes 524320 | tf_op jit(solution)/shard_map/all_to_all | solution.py:43
  429.2 9.0 %all-to-all-done.10 = bf16[64,32,128]{2,0,1:T(8,128)(2,1)} async-done(((bf16[64,32,128]{2,0,1:T(8,128)(2,1)}), bf16[64,32,128]{2,0,1:T(8,128)(2,1)}, u32[]{:S(2)}, u32[]{:S(2)}) %all-to-all-start.10) | async-done | bytes 524320 | tf_op jit(solution)/shard_map/all_to_all | solution.py:43
  468.0 15.1 %all-to-all-done.12 = bf16[64,32,128]{2,0,1:T(8,128)(2,1)} async-done(((bf16[64,32,128]{2,0,1:T(8,128)(2,1)}), bf16[64,32,128]{2,0,1:T(8,128)(2,1)}, u32[]{:S(2)}, u32[]{:S(2)}) %all-to-all-start.12) | async-done | bytes 524320 | tf_op jit(solution)/shard_map/all_to_all | solution.py:43
  489.5 10.2 %all-to-all-done.13 = bf16[64,32,128]{2,0,1:T(8,128)(2,1)} async-done(((bf16[64,32,128]{2,0,1:T(8,128)(2,1)}), bf16[64,32,128]{2,0,1:T(8,128)(2,1)}, u32[]{:S(2)}, u32[]{:S(2)}) %all-to-all-start.13) | async-done | bytes 524320 | tf_op jit(solution)/shard_map/all_to_all | solution.py:43
  506.1 10.2 %all-to-all-done.14 = bf16[64,32,128]{2,0,1:T(8,128)(2,1)} async-done(((bf16[64,32,128]{2,0,1:T(8,128)(2,1)}), bf16[64,32,128]{2,0,1:T(8,128)(2,1)}, u32[]{:S(2)}, u32[]{:S(2)}) %all-to-all-start.14) | async-done | bytes 524320 | tf_op jit(solution)/shard_map/all_to_all | solution.py:43
  593.4 263.9 %while.37 = (s32[]{:T(128)}, bf16[2,2,512,128]{3,2,0,1:T(8,128)(2,1)}, s32[2]{0:T(128)S(1)}, pred[15360]{0:T(1024)(128)(4,1)S(1)}, f32[8,4]{0,1:T(4,128)S(1)}, /...) while((s32[]{:T(128)}, ...), condition=%wide.region_5.6_spmd.clone, body=%wide.region_0.5_spmd.clone.sunk | while | flops 4522380288 | bytes 123787224 | solution.py:94
  597.2 38.8 %fusion.52 = pred[512,15360]{1,0:T(32,128)(4,1)} fusion(f32[512,4]{0,1:T(4,128)S(1)} %fusion.51, s32[15360]{0:T(1024)S(1)} %sub.161, s32[512]{0:T(512)S(1)} %add_select_fusion.3, pred[15360]{0:T(1024)(128)(4,1)S(1)} %get-tuple-element.564, pred[15360]{0:T(1024)(128)(4,1)S(1)} %get-tuple-element.553, s32[15360]{0:T(1024)S(1)} %get-tuple-element.559), kind=kOutput, calls=%fused_computation.20.clone.1 | convolution fusion | flops 432660480 | bytes 8028160 | tf_op jit(solution)/shard_map/while/body/eval_jaxpr/dot_general | solution.py:75
  636.0 88.5 %while.38 = (s32[]{:T(128)}, bf16[2,512,128]{2,1,0:T(8,128)(2,1)S(1)}, bf16[2,1024,128]{2,1,0:T(8,128)(2,1)S(1)}, s32[]{:T(128)}, bf16[2,15360,128]{2,1,0:T(8,12...) while((s32[]{:T(128)}, ...), condition=%wide.region_4.4_spmd, body=%wide.region_1.3_spmd.sunk | while | flops 4089510912 | bytes 110375024 | solution.py:92
  636.1 17.0 %fusion.54 = (f32[512]{0:T(512)S(1)}, f32[512,15360]{1,0:T(8,128)}) fusion(pred[512,15360]{1,0:T(32,128)(4,1)} %get-tuple-element.512, bf16[2,15360,128]{2,1,0:T(8,128)(2,1)} %get-tuple-element.511, s32[]{:T(128)} %get-tuple-element.498, bf16[2,1024,128]{2,1,0:T(8,128)(2,1)S(1)} %get-tuple-element.509, s32[]{:T(128)S(6)} %dynamic_slice.62, ...), kind=kOutput, calls=%fused_computation.91.clone.1 | convolution fusion | flops 2036858368 | bytes 43387908 | tf_op jit(solution)/shard_map/while/body/eval_jaxpr/while/body/eval_jaxpr/dot_general | solution.py:83
  653.1 13.1 %fusion.55 = f32[512]{0:T(512)S(1)} fusion(f32[512,15360]{1,0:T(8,128)} %get-tuple-element.487, f32[512]{0:T(512)S(1)} %get-tuple-element.488), kind=kLoop, calls=%fused_computation.6.clone.1 | loop fusion | flops 15728128 | bytes 31461376 | tf_op jit(solution)/shard_map/while/body/eval_jaxpr/while/body/eval_jaxpr/reduce_sum | solution.py:89
  666.2 14.2 %fusion.56 = bf16[2,512,128]{2,1,0:T(8,128)(2,1)S(1)} fusion(bf16[2,512,128]{2,1,0:T(8,128)(2,1)S(1)} %get-tuple-element.499, s32[]{:T(128)} %get-tuple-element.498, bf16[2,15360,128]{2,1,0:T(8,128)(2,1)} %get-tuple-element.513, f32[512,15360]{1,0:T(8,128)} %get-tuple-element.487, f32[512]{0:T(512)S(1)} %fusion.55, f32[512]{0:T(512)S(1)} %get-tuple-element.488), kind=kOutput, calls=%fused_computation.14.clone.1 | convolution fusion | flops 2036924416 | bytes 35525632 | tf_op jit(solution)/shard_map/while/body/eval_jaxpr/while/body/eval_jaxpr/dot_general | solution.py:90
  680.4 17.0 %fusion.54 = (f32[512]{0:T(512)S(1)}, f32[512,15360]{1,0:T(8,128)}) fusion(pred[512,15360]{1,0:T(32,128)(4,1)} %get-tuple-element.512, bf16[2,15360,128]{2,1,0:T(8,128)(2,1)} %get-tuple-element.511, s32[]{:T(128)} %get-tuple-element.498, bf16[2,1024,128]{2,1,0:T(8,128)(2,1)S(1)} %get-tuple-element.509, s32[]{:T(128)S(6)} %dynamic_slice.62, ...), kind=kOutput, calls=%fused_computation.91.clone.1 | convolution fusion | flops 2036858368 | bytes 43387908 | tf_op jit(solution)/shard_map/while/body/eval_jaxpr/while/body/eval_jaxpr/dot_general | solution.py:83
  697.3 13.1 %fusion.55 = f32[512]{0:T(512)S(1)} fusion(f32[512,15360]{1,0:T(8,128)} %get-tuple-element.487, f32[512]{0:T(512)S(1)} %get-tuple-element.488), kind=kLoop, calls=%fused_computation.6.clone.1 | loop fusion | flops 15728128 | bytes 31461376 | tf_op jit(solution)/shard_map/while/body/eval_jaxpr/while/body/eval_jaxpr/reduce_sum | solution.py:89
  710.4 14.2 %fusion.56 = bf16[2,512,128]{2,1,0:T(8,128)(2,1)S(1)} fusion(bf16[2,512,128]{2,1,0:T(8,128)(2,1)S(1)} %get-tuple-element.499, s32[]{:T(128)} %get-tuple-element.498, bf16[2,15360,128]{2,1,0:T(8,128)(2,1)} %get-tuple-element.513, f32[512,15360]{1,0:T(8,128)} %get-tuple-element.487, f32[512]{0:T(512)S(1)} %fusion.55, f32[512]{0:T(512)S(1)} %get-tuple-element.488), kind=kOutput, calls=%fused_computation.14.clone.1 | convolution fusion | flops 2036924416 | bytes 35525632 | tf_op jit(solution)/shard_map/while/body/eval_jaxpr/while/body/eval_jaxpr/dot_general | solution.py:90
  729.0 38.8 %fusion.52 = pred[512,15360]{1,0:T(32,128)(4,1)} fusion(f32[512,4]{0,1:T(4,128)S(1)} %fusion.51, s32[15360]{0:T(1024)S(1)} %sub.161, s32[512]{0:T(512)S(1)} %add_select_fusion.3, pred[15360]{0:T(1024)(128)(4,1)S(1)} %get-tuple-element.564, pred[15360]{0:T(1024)(128)(4,1)S(1)} %get-tuple-element.553, s32[15360]{0:T(1024)S(1)} %get-tuple-element.559), kind=kOutput, calls=%fused_computation.20.clone.1 | convolution fusion | flops 432660480 | bytes 8028160 | tf_op jit(solution)/shard_map/while/body/eval_jaxpr/dot_general | solution.py:75
  767.9 88.5 %while.38 = (s32[]{:T(128)}, bf16[2,512,128]{2,1,0:T(8,128)(2,1)S(1)}, bf16[2,1024,128]{2,1,0:T(8,128)(2,1)S(1)}, s32[]{:T(128)}, bf16[2,15360,128]{2,1,0:T(8,12...) while((s32[]{:T(128)}, ...), condition=%wide.region_4.4_spmd, body=%wide.region_1.3_spmd.sunk | while | flops 4089510912 | bytes 110375024 | solution.py:92
  767.9 17.0 %fusion.54 = (f32[512]{0:T(512)S(1)}, f32[512,15360]{1,0:T(8,128)}) fusion(pred[512,15360]{1,0:T(32,128)(4,1)} %get-tuple-element.512, bf16[2,15360,128]{2,1,0:T(8,128)(2,1)} %get-tuple-element.511, s32[]{:T(128)} %get-tuple-element.498, bf16[2,1024,128]{2,1,0:T(8,128)(2,1)S(1)} %get-tuple-element.509, s32[]{:T(128)S(6)} %dynamic_slice.62, ...), kind=kOutput, calls=%fused_computation.91.clone.1 | convolution fusion | flops 2036858368 | bytes 43387908 | tf_op jit(solution)/shard_map/while/body/eval_jaxpr/while/body/eval_jaxpr/dot_general | solution.py:83
  784.9 13.1 %fusion.55 = f32[512]{0:T(512)S(1)} fusion(f32[512,15360]{1,0:T(8,128)} %get-tuple-element.487, f32[512]{0:T(512)S(1)} %get-tuple-element.488), kind=kLoop, calls=%fused_computation.6.clone.1 | loop fusion | flops 15728128 | bytes 31461376 | tf_op jit(solution)/shard_map/while/body/eval_jaxpr/while/body/eval_jaxpr/reduce_sum | solution.py:89
  798.0 14.2 %fusion.56 = bf16[2,512,128]{2,1,0:T(8,128)(2,1)S(1)} fusion(bf16[2,512,128]{2,1,0:T(8,128)(2,1)S(1)} %get-tuple-element.499, s32[]{:T(128)} %get-tuple-element.498, bf16[2,15360,128]{2,1,0:T(8,128)(2,1)} %get-tuple-element.513, f32[512,15360]{1,0:T(8,128)} %get-tuple-element.487, f32[512]{0:T(512)S(1)} %fusion.55, f32[512]{0:T(512)S(1)} %get-tuple-element.488), kind=kOutput, calls=%fused_computation.14.clone.1 | convolution fusion | flops 2036924416 | bytes 35525632 | tf_op jit(solution)/shard_map/while/body/eval_jaxpr/while/body/eval_jaxpr/dot_general | solution.py:90
  812.2 17.0 %fusion.54 = (f32[512]{0:T(512)S(1)}, f32[512,15360]{1,0:T(8,128)}) fusion(pred[512,15360]{1,0:T(32,128)(4,1)} %get-tuple-element.512, bf16[2,15360,128]{2,1,0:T(8,128)(2,1)} %get-tuple-element.511, s32[]{:T(128)} %get-tuple-element.498, bf16[2,1024,128]{2,1,0:T(8,128)(2,1)S(1)} %get-tuple-element.509, s32[]{:T(128)S(6)} %dynamic_slice.62, ...), kind=kOutput, calls=%fused_computation.91.clone.1 | convolution fusion | flops 2036858368 | bytes 43387908 | tf_op jit(solution)/shard_map/while/body/eval_jaxpr/while/body/eval_jaxpr/dot_general | solution.py:83
  829.2 13.1 %fusion.55 = f32[512]{0:T(512)S(1)} fusion(f32[512,15360]{1,0:T(8,128)} %get-tuple-element.487, f32[512]{0:T(512)S(1)} %get-tuple-element.488), kind=kLoop, calls=%fused_computation.6.clone.1 | loop fusion | flops 15728128 | bytes 31461376 | tf_op jit(solution)/shard_map/while/body/eval_jaxpr/while/body/eval_jaxpr/reduce_sum | solution.py:89
  842.3 14.2 %fusion.56 = bf16[2,512,128]{2,1,0:T(8,128)(2,1)S(1)} fusion(bf16[2,512,128]{2,1,0:T(8,128)(2,1)S(1)} %get-tuple-element.499, s32[]{:T(128)} %get-tuple-element.498, bf16[2,15360,128]{2,1,0:T(8,128)(2,1)} %get-tuple-element.513, f32[512,15360]{1,0:T(8,128)} %get-tuple-element.487, f32[512]{0:T(512)S(1)} %fusion.55, f32[512]{0:T(512)S(1)} %get-tuple-element.488), kind=kOutput, calls=%fused_computation.14.clone.1 | convolution fusion | flops 2036924416 | bytes 35525632 | tf_op jit(solution)/shard_map/while/body/eval_jaxpr/while/body/eval_jaxpr/dot_general | solution.py:90
  859.0 19.3 %all_to_all.573 = bf16[1024,2,128]{2,1,0:T(2,128)(2,1)S(1)} all-to-all(bf16[1024,2,128]{2,1,0:T(2,128)(2,1)S(1)} %copy.199), channel_id=1, replica_groups=mesh['tm'=8,'space'=16] {'space'}, dimensions={0} | all-to-all | bytes 1048576 | tf_op jit(solution)/shard_map/all_to_all | solution.py:96
  (327 shorter events, 463.8 us)
Async XLA Ops:
  4.0 18.5 %all-to-all-start.16 = ((bf16[64,32,128]{2,0,1:T(8,128)(2,1)}), bf16[64,32,128]{2,0,1:T(8,128)(2,1)S(1)}, u32[]{:S(2)}, u32[]{:S(2)}) async-start(bf16[64,32,128]{2,0,1:T(8,128)(2,1)} %copy.168), calls=%async_computation.16 | async-start | bytes 1048576 | tf_op jit(solution)/shard_map/all_to_all | solution.py:27
  26.1 18.3 %collective-permute-start.14 = (bf16[64,32,128]{2,1,0:T(8,128)(2,1)}, bf16[64,32,128]{2,1,0:T(8,128)(2,1)S(1)}, u32[]{:S(2)}, u32[]{:S(2)}) collective-permute-start(bf16[64,32,128]{2,1,0:T(8,128)(2,1)} %bitcast.151), channel_id=1, source_target_pairs={{0,16},{16,32},{32,48},{48,64},{64,80},{80,96},{96,112},{1,17},{17... | collective-permute-start | bytes 1572872 | tf_op jit(solution)/shard_map/ppermute | solution.py:14
  42.0 17.2 %collective-permute-start.15 = (bf16[64,32,128]{2,1,0:T(8,128)(2,1)}, bf16[64,32,128]{2,1,0:T(8,128)(2,1)S(1)}, u32[]{:S(2)}, u32[]{:S(2)}) collective-permute-start(bf16[64,32,128]{2,1,0:T(8,128)(2,1)} %bitcast.151), channel_id=1, source_target_pairs={{16,0},{32,16},{48,32},{64,48},{80,64},{96,80},{112,96},{17,1},{33... | collective-permute-start | bytes 1572872 | tf_op jit(solution)/shard_map/ppermute | solution.py:14
  57.9 19.2 %collective-permute-start.16 = (bf16[64,32,128]{2,1,0:T(8,128)(2,1)}, bf16[64,32,128]{2,1,0:T(8,128)(2,1)}, u32[]{:S(2)}, u32[]{:S(2)}) collective-permute-start(bf16[64,32,128]{2,1,0:T(8,128)(2,1)} %bitcast.151), channel_id=1, source_target_pairs={{0,32},{16,48},{32,64},{48,80},{64,96},{80,112},{1,33},{17,49},{33... | collective-permute-start | bytes 1572872 | tf_op jit(solution)/shard_map/ppermute | solution.py:14
  73.8 17.9 %collective-permute-start.17 = (bf16[64,32,128]{2,1,0:T(8,128)(2,1)}, bf16[64,32,128]{2,1,0:T(8,128)(2,1)}, u32[]{:S(2)}, u32[]{:S(2)}) collective-permute-start(bf16[64,32,128]{2,1,0:T(8,128)(2,1)} %bitcast.151), channel_id=1, source_target_pairs={{32,0},{48,16},{64,32},{80,48},{96,64},{112,80},{33,1},{49,17},{65... | collective-permute-start | bytes 1572872 | tf_op jit(solution)/shard_map/ppermute | solution.py:14
  90.4 20.7 %collective-permute-start.18 = (bf16[64,32,128]{2,1,0:T(8,128)(2,1)}, bf16[64,32,128]{2,1,0:T(8,128)(2,1)}, u32[]{:S(2)}, u32[]{:S(2)}) collective-permute-start(bf16[64,32,128]{2,1,0:T(8,128)(2,1)} %bitcast.151), channel_id=1, source_target_pairs={{0,48},{16,64},{32,80},{48,96},{64,112},{1,49},{17,65},{33,81},{49... | collective-permute-start | bytes 1572872 | tf_op jit(solution)/shard_map/ppermute | solution.py:14
  107.0 17.9 %collective-permute-start.19 = (bf16[64,32,128]{2,1,0:T(8,128)(2,1)}, bf16[64,32,128]{2,1,0:T(8,128)(2,1)}, u32[]{:S(2)}, u32[]{:S(2)}) collective-permute-start(bf16[64,32,128]{2,1,0:T(8,128)(2,1)} %bitcast.151), channel_id=1, source_target_pairs={{48,0},{64,16},{80,32},{96,48},{112,64},{49,1},{65,17},{81,33},{97... | collective-permute-start | bytes 1572872 | tf_op jit(solution)/shard_map/ppermute | solution.py:14
  123.7 23.6 %collective-permute-start.20 = (bf16[64,32,128]{2,1,0:T(8,128)(2,1)}, bf16[64,32,128]{2,1,0:T(8,128)(2,1)}, u32[]{:S(2)}, u32[]{:S(2)}) collective-permute-start(bf16[64,32,128]{2,1,0:T(8,128)(2,1)} %bitcast.151), channel_id=1, source_target_pairs={{0,64},{16,80},{32,96},{48,112},{1,65},{17,81},{33,97},{49,113},{2... | collective-permute-start | bytes 1572872 | tf_op jit(solution)/shard_map/ppermute | solution.py:14
  140.3 18.3 %collective-permute-start.21 = (bf16[64,32,128]{2,1,0:T(8,128)(2,1)}, bf16[64,32,128]{2,1,0:T(8,128)(2,1)}, u32[]{:S(2)}, u32[]{:S(2)}) collective-permute-start(bf16[64,32,128]{2,1,0:T(8,128)(2,1)} %bitcast.151), channel_id=1, source_target_pairs={{64,0},{80,16},{96,32},{112,48},{65,1},{81,17},{97,33},{113,49},{6... | collective-permute-start | bytes 1572872 | tf_op jit(solution)/shard_map/ppermute | solution.py:14
  157.3 22.6 %collective-permute-start.22 = (bf16[64,32,128]{2,1,0:T(8,128)(2,1)}, bf16[64,32,128]{2,1,0:T(8,128)(2,1)}, u32[]{:S(2)}, u32[]{:S(2)}) collective-permute-start(bf16[64,32,128]{2,1,0:T(8,128)(2,1)} %bitcast.151), channel_id=1, source_target_pairs={{0,80},{16,96},{32,112},{1,81},{17,97},{33,113},{2,82},{18,98},{34... | collective-permute-start | bytes 1572872 | tf_op jit(solution)/shard_map/ppermute | solution.py:14
  173.9 18.4 %collective-permute-start.23 = (bf16[64,32,128]{2,1,0:T(8,128)(2,1)}, bf16[64,32,128]{2,1,0:T(8,128)(2,1)}, u32[]{:S(2)}, u32[]{:S(2)}) collective-permute-start(bf16[64,32,128]{2,1,0:T(8,128)(2,1)} %bitcast.151), channel_id=1, source_target_pairs={{80,0},{96,16},{112,32},{81,1},{97,17},{113,33},{82,2},{98,18},{11... | collective-permute-start | bytes 1572872 | tf_op jit(solution)/shard_map/ppermute | solution.py:14
  191.0 21.8 %collective-permute-start.24 = (bf16[64,32,128]{2,1,0:T(8,128)(2,1)}, bf16[64,32,128]{2,1,0:T(8,128)(2,1)}, u32[]{:S(2)}, u32[]{:S(2)}) collective-permute-start(bf16[64,32,128]{2,1,0:T(8,128)(2,1)} %bitcast.151), channel_id=1, source_target_pairs={{0,96},{16,112},{1,97},{17,113},{2,98},{18,114},{3,99},{19,115},{4... | collective-permute-start | bytes 1572872 | tf_op jit(solution)/shard_map/ppermute | solution.py:14
  207.6 18.4 %collective-permute-start.25 = (bf16[64,32,128]{2,1,0:T(8,128)(2,1)}, bf16[64,32,128]{2,1,0:T(8,128)(2,1)}, u32[]{:S(2)}, u32[]{:S(2)}) collective-permute-start(bf16[64,32,128]{2,1,0:T(8,128)(2,1)} %bitcast.151), channel_id=1, source_target_pairs={{96,0},{112,16},{97,1},{113,17},{98,2},{114,18},{99,3},{115,19},{1... | collective-permute-start | bytes 1572872 | tf_op jit(solution)/shard_map/ppermute | solution.py:14
  224.7 20.9 %collective-permute-start.26 = (bf16[64,32,128]{2,1,0:T(8,128)(2,1)}, bf16[64,32,128]{2,1,0:T(8,128)(2,1)}, u32[]{:S(2)}, u32[]{:S(2)}) collective-permute-start(bf16[64,32,128]{2,1,0:T(8,128)(2,1)} %bitcast.151), channel_id=1, source_target_pairs={{0,112},{1,113},{2,114},{3,115},{4,116},{5,117},{6,118},{7,119},{8... | collective-permute-start | bytes 1572872 | tf_op jit(solution)/shard_map/ppermute | solution.py:14
  241.4 18.4 %collective-permute-start.27 = (bf16[64,32,128]{2,1,0:T(8,128)(2,1)}, bf16[64,32,128]{2,1,0:T(8,128)(2,1)}, u32[]{:S(2)}, u32[]{:S(2)}) collective-permute-start(bf16[64,32,128]{2,1,0:T(8,128)(2,1)} %bitcast.151), channel_id=1, source_target_pairs={{112,0},{113,1},{114,2},{115,3},{116,4},{117,5},{118,6},{119,7},{1... | collective-permute-start | bytes 1572872 | tf_op jit(solution)/shard_map/ppermute | solution.py:14
  258.5 19.8 %collective-permute-start = (bf16[64,32,128]{2,1,0:T(8,128)(2,1)S(1)}, bf16[64,32,128]{2,1,0:T(8,128)(2,1)}, u32[]{:S(2)}, u32[]{:S(2)}) collective-permute-start(bf16[64,32,128]{2,1,0:T(8,128)(2,1)S(1)} %bitcast.199), channel_id=1, source_target_pairs={{0,16},{16,32},{32,48},{48,64},{64,80},{80,96},{96,112},{1,17},{17... | collective-permute-start | bytes 1572872 | tf_op jit(solution)/shard_map/ppermute | solution.py:14
  275.1 17.9 %collective-permute-start.1 = (bf16[64,32,128]{2,1,0:T(8,128)(2,1)S(1)}, bf16[64,32,128]{2,1,0:T(8,128)(2,1)}, u32[]{:S(2)}, u32[]{:S(2)}) collective-permute-start(bf16[64,32,128]{2,1,0:T(8,128)(2,1)S(1)} %bitcast.200), channel_id=1, source_target_pairs={{16,0},{32,16},{48,32},{64,48},{80,64},{96,80},{112,96},{17,1},{33... | collective-permute-start | bytes 1572872 | tf_op jit(solution)/shard_map/ppermute | solution.py:14
  291.7 20.5 %collective-permute-start.2 = (bf16[64,32,128]{2,1,0:T(8,128)(2,1)S(1)}, bf16[64,32,128]{2,1,0:T(8,128)(2,1)}, u32[]{:S(2)}, u32[]{:S(2)}) collective-permute-start(bf16[64,32,128]{2,1,0:T(8,128)(2,1)S(1)} %bitcast.201), channel_id=1, source_target_pairs={{0,32},{16,48},{32,64},{48,80},{64,96},{80,112},{1,33},{17,49},{33... | collective-permute-start | bytes 1572872 | tf_op jit(solution)/shard_map/ppermute | solution.py:14
  308.4 17.9 %collective-permute-start.3 = (bf16[64,32,128]{2,1,0:T(8,128)(2,1)S(1)}, bf16[64,32,128]{2,1,0:T(8,128)(2,1)}, u32[]{:S(2)}, u32[]{:S(2)}) collective-permute-start(bf16[64,32,128]{2,1,0:T(8,128)(2,1)S(1)} %bitcast.202), channel_id=1, source_target_pairs={{32,0},{48,16},{64,32},{80,48},{96,64},{112,80},{33,1},{49,17},{65... | collective-permute-start | bytes 1572872 | tf_op jit(solution)/shard_map/ppermute | solution.py:14
  325.0 20.9 %collective-permute-start.4 = (bf16[64,32,128]{2,1,0:T(8,128)(2,1)S(1)}, bf16[64,32,128]{2,1,0:T(8,128)(2,1)}, u32[]{:S(2)}, u32[]{:S(2)}) collective-permute-start(bf16[64,32,128]{2,1,0:T(8,128)(2,1)S(1)} %bitcast.203), channel_id=1, source_target_pairs={{0,48},{16,64},{32,80},{48,96},{64,112},{1,49},{17,65},{33,81},{49... | collective-permute-start | bytes 1572872 | tf_op jit(solution)/shard_map/ppermute | solution.py:14
  341.8 17.9 %collective-permute-start.5 = (bf16[64,32,128]{2,1,0:T(8,128)(2,1)S(1)}, bf16[64,32,128]{2,1,0:T(8,128)(2,1)}, u32[]{:S(2)}, u32[]{:S(2)}) collective-permute-start(bf16[64,32,128]{2,1,0:T(8,128)(2,1)S(1)} %bitcast.204), channel_id=1, source_target_pairs={{48,0},{64,16},{80,32},{96,48},{112,64},{49,1},{65,17},{81,33},{97... | collective-permute-start | bytes 1572872 | tf_op jit(solution)/shard_map/ppermute | solution.py:14
  358.4 23.6 %collective-permute-start.6 = (bf16[64,32,128]{2,1,0:T(8,128)(2,1)S(1)}, bf16[64,32,128]{2,1,0:T(8,128)(2,1)}, u32[]{:S(2)}, u32[]{:S(2)}) collective-permute-start(bf16[64,32,128]{2,1,0:T(8,128)(2,1)S(1)} %bitcast.205), channel_id=1, source_target_pairs={{0,64},{16,80},{32,96},{48,112},{1,65},{17,81},{33,97},{49,113},{2... | collective-permute-start | bytes 1572872 | tf_op jit(solution)/shard_map/ppermute | solution.py:14
  375.1 18.4 %collective-permute-start.7 = (bf16[64,32,128]{2,1,0:T(8,128)(2,1)S(1)}, bf16[64,32,128]{2,1,0:T(8,128)(2,1)}, u32[]{:S(2)}, u32[]{:S(2)}) collective-permute-start(bf16[64,32,128]{2,1,0:T(8,128)(2,1)S(1)} %bitcast.206), channel_id=1, source_target_pairs={{64,0},{80,16},{96,32},{112,48},{65,1},{81,17},{97,33},{113,49},{6... | collective-permute-start | bytes 1572872 | tf_op jit(solution)/shard_map/ppermute | solution.py:14
  392.2 22.5 %collective-permute-start.8 = (bf16[64,32,128]{2,1,0:T(8,128)(2,1)S(1)}, bf16[64,32,128]{2,1,0:T(8,128)(2,1)}, u32[]{:S(2)}, u32[]{:S(2)}) collective-permute-start(bf16[64,32,128]{2,1,0:T(8,128)(2,1)S(1)} %bitcast.207), channel_id=1, source_target_pairs={{0,80},{16,96},{32,112},{1,81},{17,97},{33,113},{2,82},{18,98},{34... | collective-permute-start | bytes 1572872 | tf_op jit(solution)/shard_map/ppermute | solution.py:14
  408.8 18.4 %collective-permute-start.9 = (bf16[64,32,128]{2,1,0:T(8,128)(2,1)S(1)}, bf16[64,32,128]{2,1,0:T(8,128)(2,1)}, u32[]{:S(2)}, u32[]{:S(2)}) collective-permute-start(bf16[64,32,128]{2,1,0:T(8,128)(2,1)S(1)} %bitcast.208), channel_id=1, source_target_pairs={{80,0},{96,16},{112,32},{81,1},{97,17},{113,33},{82,2},{98,18},{11... | collective-permute-start | bytes 1572872 | tf_op jit(solution)/shard_map/ppermute | solution.py:14
  425.9 31.3 %collective-permute-start.10 = (bf16[64,32,128]{2,1,0:T(8,128)(2,1)S(1)}, bf16[64,32,128]{2,1,0:T(8,128)(2,1)}, u32[]{:S(2)}, u32[]{:S(2)}) collective-permute-start(bf16[64,32,128]{2,1,0:T(8,128)(2,1)S(1)} %bitcast.209), channel_id=1, source_target_pairs={{0,96},{16,112},{1,97},{17,113},{2,98},{18,114},{3,99},{19,115},{4... | collective-permute-start | bytes 1572872 | tf_op jit(solution)/shard_map/ppermute | solution.py:14
  438.3 21.0 %all-to-all-start.11 = ((bf16[64,32,128]{2,0,1:T(8,128)(2,1)}), bf16[64,32,128]{2,0,1:T(8,128)(2,1)}, u32[]{:S(2)}, u32[]{:S(2)}) async-start(bf16[64,32,128]{2,0,1:T(8,128)(2,1)} %copy.158), calls=%async_computation.11 | async-start | bytes 1048576 | tf_op jit(solution)/shard_map/all_to_all | solution.py:43
  442.5 23.4 %collective-permute-start.11 = (bf16[64,32,128]{2,1,0:T(8,128)(2,1)S(1)}, bf16[64,32,128]{2,1,0:T(8,128)(2,1)}, u32[]{:S(2)}, u32[]{:S(2)}) collective-permute-start(bf16[64,32,128]{2,1,0:T(8,128)(2,1)S(1)} %bitcast.210), channel_id=1, source_target_pairs={{96,0},{112,16},{97,1},{113,17},{98,2},{114,18},{99,3},{115,19},{1... | collective-permute-start | bytes 1572872 | tf_op jit(solution)/shard_map/ppermute | solution.py:14
  447.6 39.8 %collective-permute-start.12 = (bf16[64,32,128]{2,1,0:T(8,128)(2,1)S(1)}, bf16[64,32,128]{2,1,0:T(8,128)(2,1)}, u32[]{:S(2)}, u32[]{:S(2)}) collective-permute-start(bf16[64,32,128]{2,1,0:T(8,128)(2,1)S(1)} %bitcast.211), channel_id=1, source_target_pairs={{0,112},{1,113},{2,114},{3,115},{4,116},{5,117},{6,118},{7,119},{8... | collective-permute-start | bytes 1572872 | tf_op jit(solution)/shard_map/ppermute | solution.py:14
  448.9 55.2 %collective-permute-start.13 = (bf16[64,32,128]{2,1,0:T(8,128)(2,1)S(1)}, bf16[64,32,128]{2,1,0:T(8,128)(2,1)}, u32[]{:S(2)}, u32[]{:S(2)}) collective-permute-start(bf16[64,32,128]{2,1,0:T(8,128)(2,1)S(1)} %bitcast.212), channel_id=1, source_target_pairs={{112,0},{113,1},{114,2},{115,3},{116,4},{117,5},{118,6},{119,7},{1... | collective-permute-start | bytes 1572872 | tf_op jit(solution)/shard_map/ppermute | solution.py:14
  459.2 23.8 %all-to-all-start.12 = ((bf16[64,32,128]{2,0,1:T(8,128)(2,1)}), bf16[64,32,128]{2,0,1:T(8,128)(2,1)}, u32[]{:S(2)}, u32[]{:S(2)}) async-start(bf16[64,32,128]{2,0,1:T(8,128)(2,1)} %copy.160), calls=%async_computation.12 | async-start | bytes 1048576 | tf_op jit(solution)/shard_map/all_to_all | solution.py:43
  516.3 50.9 %all-to-all-start.15 = ((bf16[64,32,128]{2,0,1:T(8,128)(2,1)}), bf16[64,32,128]{2,0,1:T(8,128)(2,1)}, u32[]{:S(2)}, u32[]{:S(2)}) async-start(bf16[64,32,128]{2,0,1:T(8,128)(2,1)} %copy.166), calls=%async_computation.15 | async-start | bytes 1048576 | tf_op jit(solution)/shard_map/all_to_all | solution.py:43
  (72 other events, 2471.5 us)
where the time goes:
time: 896 us; the launch traced here: 880 us
  waiting for transfers between devices  236 us (26%)
  starting transfers between devices  221 us (25%)
  matrix products  203 us (23%)
  local copies, waits for them, and re-layouts  143 us (16%)
  other arithmetic  53.7 us (6%)
  blocking collectives  19.3 us (2%)
    all_to_all x14, waiting for transfers between devices, on_device(): lax.all_to_all(moved_value_band, 'space', split_axis=1, concat_axis=0, ti...  105 us
    all_to_all x14, waiting for transfers between devices, on_device(): lax.all_to_all(moved_key_band, 'space', split_axis=1, concat_axis=0, tile...  102 us
    ppermute x28, starting transfers between devices, shifted(): lax.ppermute(value, axis, [(source, source + steps) for source in range(f...  87.5 us
    dot_general x2, matrix products, one_block(): jnp.dot(row_widths, level_onehot.T, precision=lax.Precision.HIGHEST)  77.5 us
    dot_general x4, matrix products, one_head(): jnp.dot(query_rows, k_head.T, preferred_element_type=jnp.float32)  67.9 us
    all_to_all x14, starting transfers between devices, on_device(): lax.all_to_all(moved_key_band, 'space', split_axis=1, concat_axis=0, tile...  61.9 us
    all_to_all x14, starting transfers between devices, on_device(): lax.all_to_all(moved_value_band, 'space', split_axis=1, concat_axis=0, ti...  58.2 us
    dot_general x4, matrix products, one_head(): jnp.dot(weights, v_head, preferred_element_type=jnp.float32)  56.6 us
  transfers between devices with their start and end apart: 59, of which 29 were waited for; matrix products, arithmetic and copies ran while one was open for 12% of the time, Pallas kernels for 0%

commit v1 on v0

v1 whole, which is shorter than its diff:
```python
import functools

import jax
import jax.numpy as jnp
from jax import lax
from jax.experimental import pallas as pl
from jax.experimental.pallas import tpu as pltpu
from jax.sharding import Mesh, PartitionSpec as P

HEADS = 32
DIM = 128
BLK = 128
LOG2E = 1.4426950408889634
SCALE = LOG2E * DIM ** -0.5
FRAMES = 8
BLOCKS = 8
BAND = 64
HALF = BAND // 2
TILE = BLOCKS * HALF
KEYS = BLOCKS * BAND
ROWS = FRAMES * TILE
OFF = -1e30
SAFE = 80.0
CHIPS = ("xl", "z1", "z0", "xh", "y")
NT = (((1,), (1,)), ((), ()))


def pack_kernel(q_ref, k_ref, v_ref, out_ref):
    for head in range(HEADS):
        cols = slice(head * DIM, (head + 1) * DIM)
        high, low = head // 8, head % 8
        keys, values = k_ref[:, cols], v_ref[:, cols]
        for half in range(2):
            dest = (high * 2 + half) * 8 + low
            out_ref[dest, 0:HALF, :] = q_ref[half * HALF:(half + 1) * HALF, cols]
            out_ref[dest, HALF:HALF + BAND, :] = keys
            out_ref[dest, HALF + BAND:, :] = values


def unpack_kernel(in_ref, out_ref):
    for head in range(HEADS):
        high, low = head // 8, head % 8
        for half in range(2):
            out_ref[half * HALF:(half + 1) * HALF, head * DIM:(head + 1) * DIM] = in_ref[(high * 2 + half) * 8 + low]


def fill_bias(w_ref, bias):
    block = lax.broadcasted_iota(jnp.int32, (1, KEYS), 1) // BAND
    bias[0] = jnp.zeros((BLOCKS, KEYS), jnp.float32)
    for level in range(4):
        for row in range(BLOCKS):
            near = jnp.abs(block - row) <= w_ref[level, row]
            bias[level + 1, row:row + 1, :] = jnp.where(near, 0.0, OFF)


def pattern(query_frame, key_frame):
    gap = jnp.abs(query_frame - key_frame)
    return (gap > 0).astype(jnp.int32) + (gap > 1).astype(jnp.int32) + (gap > 2).astype(jnp.int32) + (gap > 4).astype(jnp.int32)


def queries_of(q_ref, frame):
    return q_ref[pl.ds(frame * BLOCKS, BLOCKS), 0:HALF, :].reshape(TILE, DIM)


def keys_of(kv_ref, frame):
    return kv_ref[frame * BLOCKS:(frame + 1) * BLOCKS, HALF:HALF + BAND, :].reshape(KEYS, DIM)


def values_of(kv_ref, frame):
    return kv_ref[frame * BLOCKS:(frame + 1) * BLOCKS, HALF + BAND:, :].reshape(KEYS, DIM)


def scores_of(queries, keys, bias, query_frame, key_frame):
    scores = lax.dot_general(queries, keys, NT, preferred_element_type=jnp.float32) * SCALE
    rows = bias[pattern(query_frame, key_frame)]
    spread = jnp.broadcast_to(rows[:, None, :], (BLOCKS, HALF, KEYS)).reshape(TILE, KEYS)
    return scores + spread


def norm_top(ref, first, last):
    block = ref[:, first:last, :].astype(jnp.float32)
    return jnp.max(jnp.sum(block * block, axis=-1))


def attend_kernel(merge, w_ref, q_ref, kv_ref, *refs):
    if merge:
        before, top_before, out_ref, bias, shift = refs
    else:
        out_ref, shift, bias = refs
    fill_bias(w_ref, bias)
    bound = norm_top(q_ref, 0, HALF) * norm_top(kv_ref, HALF, HALF + BAND)
    wide = jnp.logical_not(bound * (SCALE * SCALE) <= SAFE * SAFE)
    if merge:
        wide = wide | (jnp.max(jnp.abs(top_before[...])) > 0.0)
    shift[...] = jnp.zeros((ROWS, DIM), jnp.float32)

    @pl.when(wide)
    def _():
        def tops(step, _):
            queries = queries_of(q_ref, step)
            rows = pl.ds(step * TILE, TILE)
            top = top_before[rows, :] if merge else jnp.full((TILE, DIM), OFF, jnp.float32)
            for frame in range(FRAMES):
                scores = scores_of(queries, keys_of(kv_ref, frame), bias, step, frame)
                top = jnp.maximum(top, jnp.max(scores, axis=1, keepdims=True))
            shift[rows, :] = top
            return 0

        lax.fori_loop(0, FRAMES, tops, 0)

    def body(step, _):
        queries = queries_of(q_ref, step)
        rows = pl.ds(step * TILE, TILE)
        top = shift[rows, :]
        lowered = jnp.concatenate([top] * (KEYS // DIM), axis=1)
        total = jnp.zeros((TILE, 2 * DIM), jnp.float32)
        for frame in range(FRAMES):
            scores = scores_of(queries, keys_of(kv_ref, frame), bias, step, frame)
            weights = jnp.exp2(scores - lowered).astype(jnp.bfloat16)
            values = jnp.concatenate([values_of(kv_ref, frame), jnp.ones((KEYS, DIM), jnp.bfloat16)], axis=1)
            total = total + jnp.dot(weights, values, preferred_element_type=jnp.float32)
        if merge:
            scale = jnp.exp2(top_before[rows, :] - top)
            old = before[rows, :]
            upper = total[:, :DIM] + old[:, :DIM] * scale
            lower = total[:, DIM:] + old[:, DIM:] * scale
            result = (upper / lower).astype(jnp.bfloat16)
            out_ref[pl.ds(step * BLOCKS, BLOCKS), :, :] = result.reshape(BLOCKS, HALF, DIM)
        else:
            out_ref[rows, :] = total
        return 0

    lax.fori_loop(0, FRAMES, body, 0)


def attend(widths, arrived, keyed, before=None):
    merge = before is not None
    vmem = pl.BlockSpec(memory_space=pltpu.VMEM)
    bias = pltpu.VMEM((5, BLOCKS, KEYS), jnp.float32)
    tops = jax.ShapeDtypeStruct((ROWS, DIM), jnp.float32)
    if merge:
        shape = jax.ShapeDtypeStruct((FRAMES * BLOCKS, HALF, DIM), jnp.bfloat16)
        scratch, specs = [bias, pltpu.VMEM((ROWS, DIM), jnp.float32)], vmem
    else:
        shape = [jax.ShapeDtypeStruct((ROWS, 2 * DIM), jnp.float32), tops]
        scratch, specs = [bias], [vmem, vmem]
    pairs = ROWS * FRAMES * KEYS
    return pl.pallas_call(
        functools.partial(attend_kernel, merge),
        out_shape=shape,
        in_specs=[pl.BlockSpec(memory_space=pltpu.SMEM)] + [vmem] * (4 if merge else 2),
        out_specs=specs,
        scratch_shapes=scratch,
        compiler_params=pltpu.CompilerParams(vmem_limit_bytes=50 << 20),
        cost_estimate=pl.CostEstimate(flops=pairs * DIM * 6, bytes_accessed=6 << 20, transcendentals=pairs),
    )(widths, arrived, keyed, *(before or ()))


def on_device(query, key, value, widths):
    vmem = pl.BlockSpec(memory_space=pltpu.VMEM)
    parcels = pl.pallas_call(
        pack_kernel,
        out_shape=jax.ShapeDtypeStruct((2 * HEADS, HALF + 2 * BAND, DIM), jnp.bfloat16),
        in_specs=[vmem] * 3,
        out_specs=vmem,
        compiler_params=pltpu.CompilerParams(vmem_limit_bytes=32 << 20),
        cost_estimate=pl.CostEstimate(flops=0, bytes_accessed=4 << 20, transcendentals=0),
    )(query[0], key[0], value[0])
    arrived = lax.all_to_all(parcels, CHIPS, split_axis=0, concat_axis=0, tiled=True)
    other = lax.ppermute(arrived, "c", [(0, 1), (1, 0)])
    before = attend(widths, arrived, arrived)
    result = attend(widths, arrived, other, before)
    returned = lax.all_to_all(result, CHIPS, split_axis=0, concat_axis=0, tiled=True)
    out = pl.pallas_call(
        unpack_kernel,
        out_shape=jax.ShapeDtypeStruct((BAND, HEADS * DIM), jnp.bfloat16),
        in_specs=[vmem],
        out_specs=vmem,
        compiler_params=pltpu.CompilerParams(vmem_limit_bytes=32 << 20),
        cost_estimate=pl.CostEstimate(flops=0, bytes_accessed=1 << 20, transcendentals=0),
    )(returned)
    return out[None]


def solution(mesh):
    fine = Mesh(mesh.devices.reshape(2, 2, 2, 2, 4, 2), CHIPS + ("c",))
    banded = P(("xl", "z1", "z0"), ("xh", "y", "c"), None)
    return jax.shard_map(
        on_device,
        mesh=fine,
        in_specs=(banded, banded, banded, P()),
        out_specs=banded,
        check_vma=False,
    )
```

time: 896 us -> 118 us (0.13)
  the two profiles are of different devices: /device:TPU:98 before, /device:TPU:0 now
where the time goes in v1:
time: 118 us
  blocking collectives  66 us (56%)
  Pallas kernels  45.4 us (38%)
  local copies, waits for them, and re-layouts  6.15 us (5%)
    all_to_all x1, blocking collectives, on_device(): lax.all_to_all(parcels, CHIPS, split_axis=0, concat_axis=0, tiled=True)  46.8 us
    pallas_call x2, Pallas kernels, attend(): pl.pallas_call(functools.partial(attend_kernel, merge), out_shape=shape,...  44.1 us
    all_to_all x1, blocking collectives, on_device(): lax.all_to_all(result, CHIPS, split_axis=0, concat_axis=0, tiled=True)  19.2 us
    unnamed x12, local copies, waits for them, and re-layouts  6.15 us
  transfers between devices with their start and end apart: 1, of which 0 were waited for; matrix products, arithmetic and copies ran while one was open for 0% of the time, Pallas kernels for 19%

profile of v1, /device:TPU:0, one launch (start us, length us, event | category | flops | bytes accessed | tf_op | source)
XLA Modules:
  0.0 117.6 jit_solution(14122111536987089495)
XLA Ops:
  0.0 0.0 copy-start
  0.0 1.0 copy-done
  1.0 0.0 copy-start.1
  1.0 1.0 copy-done.1
  2.1 0.0 copy-start.2
  2.1 1.0 copy-done.2
  3.1 0.4 shard_map.46
  3.5 0.0 copy-start.3
  3.5 46.8 %all_to_all.10.q_ref.kv_ref = bf16[64,160,128]{2,1,0:T(8,128)(2,1)S(1)} all-to-all(bf16[64,160,128]{2,1,0:T(8,128)(2,1)S(1)} %shard_map.46), channel_id=1, replica_groups=mesh['xl'=2,'z1'=2,'z0'=2,'xh'=2,'y'=4,'c'=2] {'xl','z1','z0','xh','y'}, dimensions={0} | all-to-all | bytes 5242880 | tf_op jit(solution)/shard_map/all_to_all | solution.py:169
  50.3 0.0 copy-start.4
  50.3 0.0 collective-permute-start
  50.3 1.5 %copy-done.4 = bf16[64,160,128]{2,1,0:T(8,128)(2,1)} copy-done((bf16[64,160,128]{2,1,0:T(8,128)(2,1)}, bf16[64,160,128]{2,1,0:T(8,128)(2,1)S(1)}, u32[]{:S(2)}) %copy-start.4) | copy-done | bytes 2621464
  51.8 0.0 copy-done.3
  51.8 22.0 %shard_map.47 = (f32[2048,256]{1,0:T(8,128)S(1)}, f32[2048,128]{1,0:T(8,128)S(1)}) custom-call(s32[4,8]{1,0:T(4,128)S(1)} %copy-done.3, bf16[64,160,128]{2,1,0:T(8,128)(2,1)} %copy-done.4, bf16[64,160,128]{2,1,0:T(8,128)(2,1)} %copy-done.4), custom_call_target="tpu_custom_call" | custom-call | flops 6442450944 | bytes 6291456 | tf_op jit(solution)/shard_map/pallas_call | solution.py:148
  73.9 0.0 collective-permute-done.kv_ref
  73.9 0.0 copy-start.5
  73.9 1.5 %copy-done.5 = bf16[64,160,128]{2,1,0:T(8,128)(2,1)} copy-done((bf16[64,160,128]{2,1,0:T(8,128)(2,1)}, bf16[64,160,128]{2,1,0:T(8,128)(2,1)S(1)}, u32[]{:S(2)}) %copy-start.5) | copy-done | bytes 2621464
  75.4 22.1 %shard_map.48 = bf16[64,32,128]{2,1,0:T(8,128)(2,1)S(1)} custom-call(s32[4,8]{1,0:T(4,128)S(1)} %copy-done.3, bf16[64,160,128]{2,1,0:T(8,128)(2,1)} %copy-done.4, bf16[64,160,128]{2,1,0:T(8,128)(2,1)} %copy-done.5, f32[2048,256]{1,0:T(8,128)S(1)} %get-tuple-element.7.refs_0_, f32[2048,128]{1,0:T(8,128)S(1)} %get-tuple-element.8.refs_1_), custom_call_target="tpu_custom_call" | custom-call | flops 6442450944 | bytes 6291456 | tf_op jit(solution)/shard_map/pallas_call | solution.py:148
  97.5 19.2 %all_to_all.11.in_ref = bf16[64,32,128]{2,1,0:T(8,128)(2,1)S(1)} all-to-all(bf16[64,32,128]{2,1,0:T(8,128)(2,1)S(1)} %shard_map.48), channel_id=1, replica_groups=mesh['xl'=2,'z1'=2,'z0'=2,'xh'=2,'y'=4,'c'=2] {'xl','z1','z0','xh','y'}, dimensions={0} | all-to-all | bytes 1048576 | tf_op jit(solution)/shard_map/all_to_all | solution.py:173
  116.7 0.9 shard_map.49
Async XLA Ops:
  0.0 1.0 copy-start
  1.0 1.0 copy-start.1
  2.1 1.0 copy-start.2
  3.5 48.3 %copy-start.3 = (s32[4,8]{1,0:T(4,128)S(1)}, s32[4,8]{1,0:T(4,128)}, u32[]{:S(2)}) copy-start(s32[4,8]{1,0:T(4,128)} %w_ref.3) | copy-start | bytes 388
  50.3 1.5 %copy-start.4 = (bf16[64,160,128]{2,1,0:T(8,128)(2,1)}, bf16[64,160,128]{2,1,0:T(8,128)(2,1)S(1)}, u32[]{:S(2)}) copy-start(bf16[64,160,128]{2,1,0:T(8,128)(2,1)S(1)} %all_to_all.10.q_ref.kv_ref) | copy-start | bytes 7864324
  50.3 23.6 %collective-permute-start = (bf16[64,160,128]{2,1,0:T(8,128)(2,1)S(1)}, bf16[64,160,128]{2,1,0:T(8,128)(2,1)S(1)}, u32[]{:S(2)}, u32[]{:S(2)}) collective-permute-start(bf16[64,160,128]{2,1,0:T(8,128)(2,1)S(1)} %all_to_all.10.q_ref.kv_ref), channel_id=1, source_target_pairs={{0,1},{1,0},{2,3},{3,2},{4,5},{5,4},{6,7},{7,6},{8,9},{9,8},{10,11... | collective-permute-start | bytes 7864328 | tf_op jit(solution)/shard_map/ppermute | solution.py:170
  73.9 1.5 %copy-start.5 = (bf16[64,160,128]{2,1,0:T(8,128)(2,1)}, bf16[64,160,128]{2,1,0:T(8,128)(2,1)S(1)}, u32[]{:S(2)}) copy-start(bf16[64,160,128]{2,1,0:T(8,128)(2,1)S(1)} %collective-permute-done.kv_ref) | copy-start | bytes 7864324

commit v2 on v1

v2 whole, which is shorter than its diff:
```python
import functools

import jax
import jax.numpy as jnp
from jax import lax
from jax.experimental import pallas as pl
from jax.experimental.pallas import tpu as pltpu
from jax.sharding import Mesh, PartitionSpec as P

HEADS = 32
DIM = 128
BLOCKS = 8
BAND = 64
FRAMES = 8
NEAR = 4
SPAN = NEAR * BAND
TILE = 2 * SPAN
ROWS = FRAMES * SPAN
STEPS = ROWS // TILE
LOG2E = 1.4426950408889634
SCALE = LOG2E * DIM ** -0.5
OFF = -1e30
SAFE = 80.0
UNROLL = 8
CUT = 6
GROUP = ("xl", "z1", "z0", "y")
SWAP = [(0, 1), (1, 0)]
NT = (((1,), (1,)), ((), ()))
VMEM = pl.BlockSpec(memory_space=pltpu.VMEM)


def pack_kernel(q_ref, k_ref, v_ref, out_ref):
    for index, ref in enumerate((q_ref, k_ref, v_ref)):
        for head in range(HEADS):
            out_ref[head, index * BAND:(index + 1) * BAND, :] = ref[0, :, head * DIM:(head + 1) * DIM]


def unpack_kernel(in_ref, out_ref):
    for head in range(HEADS):
        out_ref[0, :, head * DIM:(head + 1) * DIM] = in_ref[head]


def fill_bias(w_ref, bias, side):
    place = lax.broadcasted_iota(jnp.int32, (1, SPAN), 1) // BAND
    for far in range(2):
        block = place + (1 - side if far else side) * NEAR
        bias[far, 0] = jnp.zeros((NEAR, SPAN), jnp.float32)
        for level in range(4):
            for row in range(NEAR):
                own = side * NEAR + row
                reach = jnp.abs(block - own) <= w_ref[level, own]
                bias[far, level + 1, row:row + 1, :] = jnp.where(reach, 0.0, OFF)


def pattern(query_frame, key_frame):
    gap = jnp.abs(query_frame - key_frame)
    return (gap > 0).astype(jnp.int32) + (gap > 1).astype(jnp.int32) + (gap > 2).astype(jnp.int32) + (gap > 4).astype(jnp.int32)


def norm_top(ref, first):
    top = jnp.zeros((TILE, DIM), jnp.float32)
    ones = jnp.ones((DIM, DIM), jnp.bfloat16)
    for place in range(ref.shape[0] // BLOCKS):
        block = ref[place * BLOCKS:(place + 1) * BLOCKS, first:first + BAND, :].reshape(TILE, DIM).astype(jnp.float32)
        top = jnp.maximum(top, jnp.dot((block * block).astype(jnp.bfloat16), ones, preferred_element_type=jnp.float32))
    return jnp.max(top) * 1.02


def attend_kernel(parts, first, last, *refs):
    count = len(parts)
    q_ref, kv_refs, refs = refs[0], refs[1:1 + count], refs[1 + count:]
    if first:
        w_ref, refs = refs[0], refs[1:]
    else:
        before, top_before, facts_before, bias, refs = *refs[:4], refs[4:]
    if last:
        out_ref, refs = refs[0], refs[1:]
    elif first:
        out_ref, top_out, facts_out, bias, refs = *refs[:4], refs[4:]
    else:
        out_ref, top_out, facts_out, refs = *refs[:3], refs[3:]
    older, shift, sem = refs
    if first:
        fill_bias(w_ref, bias, lax.axis_index("xh"))
        query_top, wide_before = norm_top(q_ref, 0), None
    else:
        query_top, wide_before = jnp.max(facts_before[0:1, :]), jnp.max(facts_before[1:2, :]) > 0.0
    key_top = 0.0
    for (base, _, _), kv_ref in zip(parts, kv_refs):
        key_top = jnp.maximum(key_top, norm_top(kv_ref, base))
    wide = jnp.logical_not(query_top * key_top * (SCALE * SCALE) <= SAFE * SAFE)
    if not first:
        wide = wide | wide_before
    if not last:
        facts_out[0:1, :] = jnp.full((1, DIM), query_top, jnp.float32)
        facts_out[1:2, :] = jnp.full((1, DIM), wide.astype(jnp.float32), jnp.float32)

    tiles = []
    for (base, far, frame), kv_ref in zip(parts, kv_refs):
        for slot in range(kv_ref.shape[0] // BLOCKS):
            tiles.append((kv_ref, base, far, slot, frame + 2 * slot))

    def queries_of(step):
        return q_ref[pl.ds(step * BLOCKS, BLOCKS), 0:BAND, :].reshape(TILE, DIM)

    def scores_of(queries, step, tile):
        kv_ref, base, far, slot, frame = tile
        keys = kv_ref[slot * BLOCKS:(slot + 1) * BLOCKS, base:base + BAND, :].reshape(TILE, DIM)
        scores = lax.dot_general(queries, keys, NT, preferred_element_type=jnp.float32) * SCALE
        bands = []
        for own in range(2):
            rows = jnp.concatenate([bias[far, pattern(2 * step + own, frame + other)] for other in range(2)], axis=1)
            bands.append(jnp.broadcast_to(rows[:, None, :], (NEAR, BAND, TILE)).reshape(SPAN, TILE))
        return scores + jnp.concatenate(bands, axis=0)

    def attended(step, shifted):
        queries = queries_of(step)
        rows = pl.ds(step * TILE, TILE)
        if shifted:
            lowered = jnp.concatenate([shift[rows, :]] * (TILE // DIM), axis=1)
        total = jnp.zeros((TILE, 2 * DIM), jnp.float32) if first or shifted else before[rows, :]
        for tile in tiles:
            kv_ref, base, _, slot, _ = tile
            scores = scores_of(queries, step, tile)
            weights = jnp.exp2(scores - lowered if shifted else scores).astype(jnp.bfloat16)
            values = kv_ref[slot * BLOCKS:(slot + 1) * BLOCKS, base + BAND:base + 2 * BAND, :].reshape(TILE, DIM)
            values = jnp.concatenate([values, jnp.ones((TILE, DIM), jnp.bfloat16)], axis=1)
            total = total + jnp.dot(weights, values, preferred_element_type=jnp.float32)
        if shifted and not first:
            scale = jnp.exp2(older[rows, :] - shift[rows, :])
            total = total + before[rows, :] * jnp.concatenate([scale, scale], axis=1)
        if last:
            result = (total[:, :DIM] / total[:, DIM:]).astype(jnp.bfloat16)
            out_ref[pl.ds(step * BLOCKS, BLOCKS), :, :] = result.reshape(BLOCKS, BAND, DIM)
        else:
            out_ref[rows, :] = total

    @pl.when(jnp.logical_not(wide))
    def _():
        unrolled = min(STEPS, max(1, UNROLL // len(tiles)))

        def body(group, _):
            for step in range(unrolled):
                attended(group * unrolled + step, False)
            return 0

        lax.fori_loop(0, STEPS // unrolled, body, 0)

    @pl.when(wide)
    def _():
        if first:
            older[...] = jnp.full((ROWS, DIM), OFF, jnp.float32)
        else:
            older[...] = jnp.zeros((ROWS, DIM), jnp.float32)

            @pl.when(wide_before)
            def _():
                copy = pltpu.make_async_copy(top_before, older, sem)
                copy.start()
                copy.wait()

        def body(step, _):
            queries = queries_of(step)
            rows = pl.ds(step * TILE, TILE)
            top = older[rows, :]
            for tile in tiles:
                top = jnp.maximum(top, jnp.max(scores_of(queries, step, tile), axis=1, keepdims=True))
            shift[rows, :] = top
            attended(step, True)
            return 0

        lax.fori_loop(0, STEPS, body, 0)
        if not last:
            copy = pltpu.make_async_copy(shift, top_out, sem)
            copy.start()
            copy.wait()


def attend(arrived, keyed, parts, widths=None, before=(), last=False):
    first = not before
    anywhere, scalars = pl.BlockSpec(memory_space=pl.ANY), pl.BlockSpec(memory_space=pltpu.SMEM)
    extra = [widths] if first else list(before)
    if last:
        shape, specs = jax.ShapeDtypeStruct((HEADS, BAND, DIM), jnp.bfloat16), VMEM
    else:
        shape = [
            jax.ShapeDtypeStruct((ROWS, 2 * DIM), jnp.float32),
            jax.ShapeDtypeStruct((ROWS, DIM), jnp.float32),
            jax.ShapeDtypeStruct((8, DIM), jnp.float32),
        ]
        specs = [VMEM, anywhere, VMEM]
        if first:
            shape.append(jax.ShapeDtypeStruct((2, 5, NEAR, SPAN), jnp.float32))
            specs.append(VMEM)
    pairs = ROWS * TILE * sum(array.shape[0] // BLOCKS for array in keyed)
    return pl.pallas_call(
        functools.partial(attend_kernel, parts, first, last),
        out_shape=shape,
        in_specs=[VMEM] * (1 + len(keyed)) + ([scalars] if first else [VMEM, anywhere, VMEM, VMEM]),
        out_specs=specs,
        scratch_shapes=[
            pltpu.VMEM((ROWS, DIM), jnp.float32),
            pltpu.VMEM((ROWS, DIM), jnp.float32),
            pltpu.SemaphoreType.DMA,
        ],
        compiler_params=pltpu.CompilerParams(vmem_limit_bytes=28 << 20),
        cost_estimate=pl.CostEstimate(flops=pairs * DIM * 8, bytes_accessed=6 << 20, transcendentals=pairs),
    )(arrived, *keyed, *extra)


def on_device(query, key, value, widths):
    parcels = pl.pallas_call(
        pack_kernel,
        out_shape=jax.ShapeDtypeStruct((HEADS, 3 * BAND, DIM), jnp.bfloat16),
        in_specs=[VMEM] * 3,
        out_specs=VMEM,
        compiler_params=pltpu.CompilerParams(vmem_limit_bytes=62 << 20),
        cost_estimate=pl.CostEstimate(flops=0, bytes_accessed=4 << 20, transcendentals=0),
    )(query, key, value)
    arrived = lax.all_to_all(parcels, GROUP, split_axis=0, concat_axis=0, tiled=True)
    own = arrived[:, BAND:, :]
    across_low, across_high = (lax.ppermute(part, "xh", SWAP) for part in (own[:CUT * NEAR], own[CUT * NEAR:]))
    beside = lax.ppermute(own, "c", SWAP)
    near, far_low, far_high = (0, 0, 0), (0, 1, 0), (0, 1, CUT)

    def after(state, array):
        return lax.optimization_barrier((tuple(state), array))

    *state, bias = attend(arrived, [arrived], [(BAND, 0, 0)], widths)

    def step(keyed, parts, state, last=False):
        return attend(arrived, keyed, parts, None, (*state, bias), last)

    state = step([beside], [near], state)
    state, across_low = after(state, across_low)
    fourth_low = lax.ppermute(across_low, "c", SWAP)
    state = step([across_low], [far_low], state)
    state = step([fourth_low], [far_low], state)
    state, across_high = after(state, across_high)
    fourth_high = lax.ppermute(across_high, "c", SWAP)
    state = step([across_high], [far_high], state)
    result = step([fourth_high], [far_high], state, True)
    returned = lax.all_to_all(result, GROUP, split_axis=0, concat_axis=0, tiled=True)
    return pl.pallas_call(
        unpack_kernel,
        out_shape=jax.ShapeDtypeStruct((1, BAND, HEADS * DIM), jnp.bfloat16),
        in_specs=[VMEM],
        out_specs=VMEM,
        compiler_params=pltpu.CompilerParams(vmem_limit_bytes=32 << 20),
        cost_estimate=pl.CostEstimate(flops=0, bytes_accessed=1 << 20, transcendentals=0),
    )(returned)


def solution(mesh):
    fine = Mesh(mesh.devices.reshape(2, 2, 2, 2, 4, 2), ("xl", "z1", "z0", "xh", "y", "c"))
    banded = P(("xl", "z1", "z0"), ("xh", "y", "c"), None)
    return jax.shard_map(
        on_device,
        mesh=fine,
        in_specs=(banded, banded, banded, P()),
        out_specs=banded,
        check_vma=False,
    )
```

time: 118 us -> 101 us (0.86)
  blocking collectives: 66 us -> 48.1 us
  local copies, waits for them, and re-layouts: 6.15 us -> 0.16 us
  starting transfers between devices: 0.01 us -> 4.35 us
  Pallas kernels: 45.4 us -> 47.7 us
    all_to_all x2, blocking collectives: 66 us -> 48.1 us  [the longest x1 32.2 us: on_device(): lax.all_to_all(parcels, GROUP, split_axis=0, concat_axis=0, tiled=True)]
    unnamed x12 -> x2, local copies, waits for them, and re-layouts: 6.15 us -> 0.01 us
    ppermute x1 -> x5, starting transfers between devices: 0.01 us -> 4.35 us  [the longest x2 3.69 us: on_device(): lax.ppermute(part, 'xh', SWAP)]
    pallas_call x4 -> x8, Pallas kernels: 45.4 us -> 47.7 us  [the longest x6 44 us: attend(): pl.pallas_call(functools.partial(attend_kernel, parts, first, last), out_...]
  transfers between devices with their start and end apart: 1 -> 5, of which waited for: 0 -> 0; matrix products, arithmetic and copies ran while one was open for 0% -> 0% of each run, Pallas kernels for 19% -> 40%
where the time goes in v2:
time: 101 us; the launch traced here: 100 us
  blocking collectives  48.1 us (48%)
  Pallas kernels  47.7 us (47%)
  starting transfers between devices  4.35 us (4%)
    pallas_call x6, Pallas kernels, attend(): pl.pallas_call(functools.partial(attend_kernel, parts, first, last), out_...  44 us
    all_to_all x1, blocking collectives, on_device(): lax.all_to_all(parcels, GROUP, split_axis=0, concat_axis=0, tiled=True)  32.2 us
    all_to_all x1, blocking collectives, on_device(): lax.all_to_all(result, GROUP, split_axis=0, concat_axis=0, tiled=True)  15.9 us
    ppermute x2, starting transfers between devices, on_device(): lax.ppermute(part, 'xh', SWAP)  3.69 us
    pallas_call x1, Pallas kernels, on_device(): pl.pallas_call(pack_kernel, out_shape=jax.ShapeDtypeStruct((HEADS, 3 * BA...  2.78 us
  transfers between devices with their start and end apart: 5, of which 0 were waited for; matrix products, arithmetic and copies ran while one was open for 0% of the time, Pallas kernels for 40%

profile of v2, /device:TPU:0, one launch (start us, length us, event | category | flops | bytes accessed | tf_op | source)
XLA Modules:
  0.0 100.4 jit_solution(7630265717312382077)
XLA Ops:
  0.0 2.8 %shard_map.46 = bf16[32,192,128]{2,1,0:T(8,128)(2,1)} custom-call(bf16[1,64,4096]{2,1,0:T(8,128)(2,1)} %q_ref.1, bf16[1,64,4096]{2,1,0:T(8,128)(2,1)} %k_ref.1, bf16[1,64,4096]{2,1,0:T(8,128)(2,1)} %v_ref.1), custom_call_target="tpu_custom_call" | custom-call | bytes 4194304 | tf_op jit(solution)/shard_map/pallas_call | solution.py:212
  2.8 32.2 %all_to_all.10.refs_0_.refs_1_ = bf16[32,192,128]{2,1,0:T(8,128)(2,1)S(1)} all-to-all(bf16[32,192,128]{2,1,0:T(8,128)(2,1)} %shard_map.46), channel_id=1, replica_groups=mesh['xl'=2,'z1'=2,'z0'=2,'xh'=2,'y'=4,'c'=2] {'xl','z1','z0','y'}, dimensions={0} | all-to-all | bytes 3145728 | tf_op jit(solution)/shard_map/all_to_all | solution.py:220
  35.0 0.0 copy-start
  35.0 0.1 slice.14
  35.1 0.1 collective-permute-start
  35.2 0.1 slice.15
  35.3 2.8 %collective-permute-start.1 = (bf16[24,128,128]{2,1,0:T(8,128)(2,1)S(1)}, bf16[24,128,128]{2,1,0:T(8,128)(2,1)S(1)}, u32[]{:S(2)}, u32[]{:S(2)}) collective-permute-start(bf16[24,128,128]{2,1,0:T(8,128)(2,1)S(1)} %slice.15), channel_id=1, source_target_pairs={{0,8},{8,0},{1,9},{9,1},{2,10},{10,2},{3,11},{11,3},{4,12},{12,4},... | collective-permute-start | bytes 2359304 | tf_op jit(solution)/shard_map/ppermute | solution.py:222
  38.1 0.0 copy-done
  38.1 10.5 %shard_map.47 = (f32[2048,256]{1,0:T(8,128)S(1)}, f32[2048,128]{1,0:T(8,128)S(1)}, f32[8,128]{1,0:T(8,128)S(1)}, f32[2,5,4,256]{3,2,1,0:T(4,128)S(1)}) custom-call(bf16[32,192,128]{2,1,0:T(8,128)(2,1)S(1)} %all_to_all.10.refs_0_.refs_1_, bf16[32,192,128]{2,1,0:T(8,128)(2,1)S(1)} %all_to_all.10.refs_0_.refs_1_, s32[4,8]{1,0:T(4,128)S(1)} %copy-done), custom_call_target="tpu_custom_call" | custom-call | flops 4294967296 | bytes 6291456 | tf_op jit(solution)/shard_map/pallas_call | solution.py:196
  48.6 0.0 collective-permute-done.refs_1_
  48.6 9.9 %shard_map.48 = (f32[2048,256]{1,0:T(8,128)S(1)}, f32[2048,128]{1,0:T(8,128)S(1)}, f32[8,128]{1,0:T(8,128)S(1)}) custom-call(bf16[32,192,128]{2,1,0:T(8,128)(2,1)S(1)} %all_to_all.10.refs_0_.refs_1_, bf16[32,128,128]{2,1,0:T(8,128)(2,1)S(1)} %collective-permute-done.refs_1_, f32[2048,256]{1,0:T(8,128)S(1)} %get-tuple-element.29.refs_2_, ...), custom_call_target="tpu_custom_call" | custom-call | flops 4294967296 | bytes 6291456 | tf_op jit(solution)/shard_map/pallas_call | solution.py:196
  58.5 0.0 collective-permute-done.1.refs_1_
  58.5 0.5 collective-permute-start.2
  59.0 0.9 collective-permute-start.3
  59.9 8.1 %shard_map.49 = (f32[2048,256]{1,0:T(8,128)S(1)}, f32[2048,128]{1,0:T(8,128)S(1)}, f32[8,128]{1,0:T(8,128)S(1)}) custom-call(bf16[32,192,128]{2,1,0:T(8,128)(2,1)S(1)} %all_to_all.10.refs_0_.refs_1_, bf16[24,128,128]{2,1,0:T(8,128)(2,1)S(1)} %collective-permute-done.1.refs_1_, f32[2048,256]{1,0:T(8,128)S(1)} %get-tuple-element.37.refs_2_, ...), custom_call_target="tpu_custom_call" | custom-call | flops 3221225472 | bytes 6291456 | tf_op jit(solution)/shard_map/pallas_call | solution.py:196
  68.0 0.0 collective-permute-done.2.refs_1_
  68.0 8.1 %shard_map.50 = (f32[2048,256]{1,0:T(8,128)S(1)}, f32[2048,128]{1,0:T(8,128)S(1)}, f32[8,128]{1,0:T(8,128)S(1)}) custom-call(bf16[32,192,128]{2,1,0:T(8,128)(2,1)S(1)} %all_to_all.10.refs_0_.refs_1_, bf16[24,128,128]{2,1,0:T(8,128)(2,1)S(1)} %collective-permute-done.2.refs_1_, f32[2048,256]{1,0:T(8,128)S(1)} %get-tuple-element.40.refs_2_, ...), custom_call_target="tpu_custom_call" | custom-call | flops 3221225472 | bytes 6291456 | tf_op jit(solution)/shard_map/pallas_call | solution.py:196
  76.2 0.0 collective-permute-done.3.refs_1_
  76.2 0.1 collective-permute-start.4
  76.3 3.7 %shard_map.51 = (f32[2048,256]{1,0:T(8,128)S(1)}, f32[2048,128]{1,0:T(8,128)S(1)}, f32[8,128]{1,0:T(8,128)S(1)}) custom-call(bf16[32,192,128]{2,1,0:T(8,128)(2,1)S(1)} %all_to_all.10.refs_0_.refs_1_, bf16[8,128,128]{2,1,0:T(8,128)(2,1)S(1)} %collective-permute-done.3.refs_1_, f32[2048,256]{1,0:T(8,128)S(1)} %get-tuple-element.47.refs_2_, ...), custom_call_target="tpu_custom_call" | custom-call | flops 1073741824 | bytes 6291456 | tf_op jit(solution)/shard_map/pallas_call | solution.py:196
  80.0 0.0 collective-permute-done.4.refs_1_
  80.0 3.7 %shard_map.52 = bf16[32,64,128]{2,1,0:T(8,128)(2,1)S(1)} custom-call(bf16[32,192,128]{2,1,0:T(8,128)(2,1)S(1)} %all_to_all.10.refs_0_.refs_1_, bf16[8,128,128]{2,1,0:T(8,128)(2,1)S(1)} %collective-permute-done.4.refs_1_, f32[2048,256]{1,0:T(8,128)S(1)} %get-tuple-element.50.refs_2_, f32[2048,128]{1,0:T(8,128)S(1)} %get-tuple-element.51.refs_3_, ...), custom_call_target="tpu_custom_call" | custom-call | flops 1073741824 | bytes 6291456 | tf_op jit(solution)/shard_map/pallas_call | solution.py:196
  83.7 15.9 %all_to_all.11.in_ref = bf16[32,64,128]{2,1,0:T(8,128)(2,1)S(1)} all-to-all(bf16[32,64,128]{2,1,0:T(8,128)(2,1)S(1)} %shard_map.52), channel_id=1, replica_groups=mesh['xl'=2,'z1'=2,'z0'=2,'xh'=2,'y'=4,'c'=2] {'xl','z1','z0','y'}, dimensions={0} | all-to-all | bytes 1048576 | tf_op jit(solution)/shard_map/all_to_all | solution.py:243
  99.5 0.9 shard_map.53
  (1 shorter events, 0.0 us)
Async XLA Ops:
  35.0 3.1 %copy-start = (s32[4,8]{1,0:T(4,128)S(1)}, s32[4,8]{1,0:T(4,128)}, u32[]{:S(2)}) copy-start(s32[4,8]{1,0:T(4,128)} %refs_2_.1) | copy-start | bytes 388
  35.1 13.5 %collective-permute-start = (bf16[32,128,128]{2,1,0:T(8,128)(2,1)S(1)}, bf16[32,128,128]{2,1,0:T(8,128)(2,1)S(1)}, u32[]{:S(2)}, u32[]{:S(2)}) collective-permute-start(bf16[32,128,128]{2,1,0:T(8,128)(2,1)S(1)} %slice.14), channel_id=1, source_target_pairs={{0,1},{1,0},{2,3},{3,2},{4,5},{5,4},{6,7},{7,6},{8,9},{9,8},{10,11... | collective-permute-start | bytes 3145736 | tf_op jit(solution)/shard_map/ppermute | solution.py:223
  35.3 23.2 %collective-permute-start.1 = (bf16[24,128,128]{2,1,0:T(8,128)(2,1)S(1)}, bf16[24,128,128]{2,1,0:T(8,128)(2,1)S(1)}, u32[]{:S(2)}, u32[]{:S(2)}) collective-permute-start(bf16[24,128,128]{2,1,0:T(8,128)(2,1)S(1)} %slice.15), channel_id=1, source_target_pairs={{0,8},{8,0},{1,9},{9,1},{2,10},{10,2},{3,11},{11,3},{4,12},{12,4},... | collective-permute-start | bytes 2359304 | tf_op jit(solution)/shard_map/ppermute | solution.py:222
  58.5 9.5 %collective-permute-start.2 = (bf16[24,128,128]{2,1,0:T(8,128)(2,1)S(1)}, bf16[24,128,128]{2,1,0:T(8,128)(2,1)S(1)}, u32[]{:S(2)}, u32[]{:S(2)}) collective-permute-start(bf16[24,128,128]{2,1,0:T(8,128)(2,1)S(1)} %collective-permute-done.1.refs_1_), channel_id=1, source_target_pairs={{0,1},{1,0},{2,3},{3,2},{4,5},{5,4},{6,7},{7,6},{8,9},{9,8},{10,11... | collective-permute-start | bytes 2359304 | tf_op jit(solution)/shard_map/ppermute | solution.py:236
  59.0 17.2 %collective-permute-start.3 = (bf16[8,128,128]{2,1,0:T(8,128)(2,1)S(1)}, bf16[8,128,128]{2,1,0:T(8,128)(2,1)S(1)}, u32[]{:S(2)}, u32[]{:S(2)}) collective-permute-start(bf16[8,128,128]{2,1,0:T(8,128)(2,1)S(1)} %slice.16), channel_id=1, source_target_pairs={{0,8},{8,0},{1,9},{9,1},{2,10},{10,2},{3,11},{11,3},{4,12},{12,4},... | collective-permute-start | bytes 786440 | tf_op jit(solution)/shard_map/ppermute | solution.py:222
  76.2 3.8 %collective-permute-start.4 = (bf16[8,128,128]{2,1,0:T(8,128)(2,1)S(1)}, bf16[8,128,128]{2,1,0:T(8,128)(2,1)S(1)}, u32[]{:S(2)}, u32[]{:S(2)}) collective-permute-start(bf16[8,128,128]{2,1,0:T(8,128)(2,1)S(1)} %collective-permute-done.3.refs_1_), channel_id=1, source_target_pairs={{0,1},{1,0},{2,3},{3,2},{4,5},{5,4},{6,7},{7,6},{8,9},{9,8},{10,11... | collective-permute-start | bytes 786440 | tf_op jit(solution)/shard_map/ppermute | solution.py:240

commit v3 on v2

--- a/solution.py
+++ b/solution.py
@@ -21,18 +21,34 @@
 SCALE = LOG2E * DIM ** -0.5
 OFF = -1e30
 SAFE = 80.0
-UNROLL = 8
-CUT = 6
+PAIR = 4
+PARTS = 2
+STRIP = BAND // PARTS
+CUT = 3
 GROUP = ("xl", "z1", "z0", "y")
 SWAP = [(0, 1), (1, 0)]
 NT = (((1,), (1,)), ((), ()))
 VMEM = pl.BlockSpec(memory_space=pltpu.VMEM)
 
 
-def pack_kernel(q_ref, k_ref, v_ref, out_ref):
-    for index, ref in enumerate((q_ref, k_ref, v_ref)):
+def pack_kernel(q_ref, k_ref, v_ref, out_ref, held, ready, came, left):
+    pieces = [(index, part) for index in range(3) for part in range(PARTS)]
+    arrivals, departures = [], []
+    for index, part in pieces:
+        rows = slice(part * STRIP, (part + 1) * STRIP)
+        ref = (q_ref, k_ref, v_ref)[index]
+        arrivals.append(pltpu.make_async_copy(ref.at[0, rows, :], held.at[index, rows, :], came.at[index, part]))
+        arrivals[-1].start()
+    for (index, part), arrival in zip(pieces, arrivals):
+        arrival.wait()
+        first = part * STRIP
+        target = slice(index * BAND + first, index * BAND + first + STRIP)
         for head in range(HEADS):
-            out_ref[head, index * BAND:(index + 1) * BAND, :] = ref[0, :, head * DIM:(head + 1) * DIM]
+            ready[head, target, :] = held[index, first:first + STRIP, head * DIM:(head + 1) * DIM]
+        departures.append(pltpu.make_async_copy(ready.at[:, target, :], out_ref.at[:, target, :], left.at[index, part]))
+        departures[-1].start()
+    for departure in departures:
+        departure.wait()
 
 
 def unpack_kernel(in_ref, out_ref):
@@ -58,10 +74,10 @@
 
 
 def norm_top(ref, first):
-    top = jnp.zeros((TILE, DIM), jnp.float32)
+    top = jnp.zeros((SPAN, DIM), jnp.float32)
     ones = jnp.ones((DIM, DIM), jnp.bfloat16)
-    for place in range(ref.shape[0] // BLOCKS):
-        block = ref[place * BLOCKS:(place + 1) * BLOCKS, first:first + BAND, :].reshape(TILE, DIM).astype(jnp.float32)
+    for frame in range(ref.shape[0] // NEAR):
+        block = ref[frame * NEAR:(frame + 1) * NEAR, first:first + BAND, :].reshape(SPAN, DIM).astype(jnp.float32)
         top = jnp.maximum(top, jnp.dot((block * block).astype(jnp.bfloat16), ones, preferred_element_type=jnp.float32))
     return jnp.max(top) * 1.02
 
@@ -97,54 +113,57 @@
 
     tiles = []
     for (base, far, frame), kv_ref in zip(parts, kv_refs):
-        for slot in range(kv_ref.shape[0] // BLOCKS):
-            tiles.append((kv_ref, base, far, slot, frame + 2 * slot))
+        count = kv_ref.shape[0] // NEAR
+        for slot in range(0, count, 2):
+            tiles.append((kv_ref, base, far, slot, min(2, count - slot), frame + slot))
+
+    def cut(tile, first):
+        kv_ref, _, _, slot, width, _ = tile
+        return kv_ref[slot * NEAR:(slot + width) * NEAR, first:first + BAND, :].reshape(width * SPAN, DIM)
 
     def queries_of(step):
         return q_ref[pl.ds(step * BLOCKS, BLOCKS), 0:BAND, :].reshape(TILE, DIM)
 
     def scores_of(queries, step, tile):
-        kv_ref, base, far, slot, frame = tile
-        keys = kv_ref[slot * BLOCKS:(slot + 1) * BLOCKS, base:base + BAND, :].reshape(TILE, DIM)
+        _, base, far, _, width, frame = tile
+        keys = cut(tile, base)
         scores = lax.dot_general(queries, keys, NT, preferred_element_type=jnp.float32) * SCALE
         bands = []
         for own in range(2):
-            rows = jnp.concatenate([bias[far, pattern(2 * step + own, frame + other)] for other in range(2)], axis=1)
-            bands.append(jnp.broadcast_to(rows[:, None, :], (NEAR, BAND, TILE)).reshape(SPAN, TILE))
+            rows = jnp.concatenate([bias[far, pattern(2 * step + own, frame + other)] for other in range(width)], axis=1)
+            bands.append(jnp.broadcast_to(rows[:, None, :], (NEAR, BAND, width * SPAN)).reshape(SPAN, width * SPAN))
         return scores + jnp.concatenate(bands, axis=0)
 
-    def attended(step, shifted):
-        queries = queries_of(step)
-        rows = pl.ds(step * TILE, TILE)
-        if shifted:
-            lowered = jnp.concatenate([shift[rows, :]] * (TILE // DIM), axis=1)
-        total = jnp.zeros((TILE, 2 * DIM), jnp.float32) if first or shifted else before[rows, :]
+    def attended(steps, shifted):
+        queries = [queries_of(step) for step in steps]
+        spans = [pl.ds(step * TILE, TILE) for step in steps]
+        totals = [jnp.zeros((TILE, 2 * DIM), jnp.float32) if first or shifted else before[rows, :] for rows in spans]
         for tile in tiles:
-            kv_ref, base, _, slot, _ = tile
-            scores = scores_of(queries, step, tile)
-            weights = jnp.exp2(scores - lowered if shifted else scores).astype(jnp.bfloat16)
-            values = kv_ref[slot * BLOCKS:(slot + 1) * BLOCKS, base + BAND:base + 2 * BAND, :].reshape(TILE, DIM)
-            values = jnp.concatenate([values, jnp.ones((TILE, DIM), jnp.bfloat16)], axis=1)
-            total = total + jnp.dot(weights, values, preferred_element_type=jnp.float32)
-        if shifted and not first:
-            scale = jnp.exp2(older[rows, :] - shift[rows, :])
-            total = total + before[rows, :] * jnp.concatenate([scale, scale], axis=1)
-        if last:
-            result = (total[:, :DIM] / total[:, DIM:]).astype(jnp.bfloat16)
-            out_ref[pl.ds(step * BLOCKS, BLOCKS), :, :] = result.reshape(BLOCKS, BAND, DIM)
-        else:
-            out_ref[rows, :] = total
+            values = cut(tile, tile[1] + BAND)
+            values = jnp.concatenate([values, jnp.ones(values.shape, jnp.bfloat16)], axis=1)
+            for index, step in enumerate(steps):
+                scores = scores_of(queries[index], step, tile)
+                if shifted:
+                    scores = scores - jnp.concatenate([shift[spans[index], :]] * (scores.shape[1] // DIM), axis=1)
+                weights = jnp.exp2(scores).astype(jnp.bfloat16)
+                totals[index] = totals[index] + jnp.dot(weights, values, preferred_element_type=jnp.float32)
+        for step, rows, total in zip(steps, spans, totals):
+            if shifted and not first:
+                scale = jnp.exp2(older[rows, :] - shift[rows, :])
+                total = total + before[rows, :] * jnp.concatenate([scale, scale], axis=1)
+            if last:
+                result = (total[:, :DIM] / total[:, DIM:]).astype(jnp.bfloat16)
+                out_ref[pl.ds(step * BLOCKS, BLOCKS), :, :] = result.reshape(BLOCKS, BAND, DIM)
+            else:
+                out_ref[rows, :] = total
 
     @pl.when(jnp.logical_not(wide))
     def _():
-        unrolled = min(STEPS, max(1, UNROLL // len(tiles)))
-
         def body(group, _):
-            for step in range(unrolled):
-                attended(group * unrolled + step, False)
+            attended([group * PAIR + step for step in range(PAIR)], False)
             return 0
 
-        lax.fori_loop(0, STEPS // unrolled, body, 0)
+        lax.fori_loop(0, STEPS // PAIR, body, 0)
 
     @pl.when(wide)
     def _():
@@ -166,7 +185,7 @@
             for tile in tiles:
                 top = jnp.maximum(top, jnp.max(scores_of(queries, step, tile), axis=1, keepdims=True))
             shift[rows, :] = top
-            attended(step, True)
+            attended([step], True)
             return 0
 
         lax.fori_loop(0, STEPS, body, 0)
@@ -192,7 +211,7 @@
         if first:
             shape.append(jax.ShapeDtypeStruct((2, 5, NEAR, SPAN), jnp.float32))
             specs.append(VMEM)
-    pairs = ROWS * TILE * sum(array.shape[0] // BLOCKS for array in keyed)
+    pairs = ROWS * TILE * sum(array.shape[0] for array in keyed) // BLOCKS
     return pl.pallas_call(
         functools.partial(attend_kernel, parts, first, last),
         out_shape=shape,
@@ -212,8 +231,14 @@
     parcels = pl.pallas_call(
         pack_kernel,
         out_shape=jax.ShapeDtypeStruct((HEADS, 3 * BAND, DIM), jnp.bfloat16),
-        in_specs=[VMEM] * 3,
-        out_specs=VMEM,
+        in_specs=[pl.BlockSpec(memory_space=pl.ANY)] * 3,
+        out_specs=pl.BlockSpec(memory_space=pl.ANY),
+        scratch_shapes=[
+            pltpu.VMEM((3, BAND, HEADS * DIM), jnp.bfloat16),
+            pltpu.VMEM((HEADS, 3 * BAND, DIM), jnp.bfloat16),
+            pltpu.SemaphoreType.DMA((3, PARTS)),
+            pltpu.SemaphoreType.DMA((3, PARTS)),
+        ],
         compiler_params=pltpu.CompilerParams(vmem_limit_bytes=62 << 20),
         cost_estimate=pl.CostEstimate(flops=0, bytes_accessed=4 << 20, transcendentals=0),
     )(query, key, value)

time: 101 us -> 101 us (level)
    pallas_call x6, Pallas kernels: 44 us -> 45.3 us  [attend(): pl.pallas_call(functools.partial(attend_kernel, parts, first, last), out_...]
  transfers between devices with their start and end apart: 5 -> 5, of which waited for: 0 -> 0; matrix products, arithmetic and copies ran while one was open for 0% -> 0% of each run, Pallas kernels for 40% -> 38%
where the time goes in v3:
time: 101 us
  Pallas kernels  48.4 us (48%)
  blocking collectives  47.6 us (47%)
  starting transfers between devices  4.43 us (4%)
    pallas_call x6, Pallas kernels, attend(): pl.pallas_call(functools.partial(attend_kernel, parts, first, last), out_...  45.3 us
    all_to_all x1, blocking collectives, on_device(): lax.all_to_all(parcels, GROUP, split_axis=0, concat_axis=0, tiled=True)  32.2 us
    all_to_all x1, blocking collectives, on_device(): lax.all_to_all(result, GROUP, split_axis=0, concat_axis=0, tiled=True)  15.4 us
    ppermute x2, starting transfers between devices, on_device(): lax.ppermute(part, 'xh', SWAP)  3.69 us
    pallas_call x1, Pallas kernels, on_device(): pl.pallas_call(pack_kernel, out_shape=jax.ShapeDtypeStruct((HEADS, 3 * BA...  2.25 us
  transfers between devices with their start and end apart: 5, of which 0 were waited for; matrix products, arithmetic and copies ran while one was open for 0% of the time, Pallas kernels for 38%

profile of v3, /device:TPU:0, one launch (start us, length us, event | category | flops | bytes accessed | tf_op | source)
XLA Modules:
  0.0 100.8 jit_solution(8297154282440938645)
XLA Ops:
  0.0 2.2 %shard_map.46 = bf16[32,192,128]{2,1,0:T(8,128)(2,1)} custom-call(bf16[1,64,4096]{2,1,0:T(8,128)(2,1)} %q_ref.1, bf16[1,64,4096]{2,1,0:T(8,128)(2,1)} %k_ref.1, bf16[1,64,4096]{2,1,0:T(8,128)(2,1)} %v_ref.1), custom_call_target="tpu_custom_call" | custom-call | bytes 4194304 | tf_op jit(solution)/shard_map/pallas_call | solution.py:231
  2.3 32.2 %all_to_all.10.refs_0_.refs_1_ = bf16[32,192,128]{2,1,0:T(8,128)(2,1)S(1)} all-to-all(bf16[32,192,128]{2,1,0:T(8,128)(2,1)} %shard_map.46), channel_id=1, replica_groups=mesh['xl'=2,'z1'=2,'z0'=2,'xh'=2,'y'=4,'c'=2] {'xl','z1','z0','y'}, dimensions={0} | all-to-all | bytes 3145728 | tf_op jit(solution)/shard_map/all_to_all | solution.py:245
  34.5 0.0 copy-start
  34.5 0.1 slice.14
  34.6 0.1 collective-permute-start
  34.7 2.8 %collective-permute-start.1 = (bf16[12,128,128]{2,1,0:T(8,128)(2,1)S(1)}, bf16[12,128,128]{2,1,0:T(8,128)(2,1)S(1)}, u32[]{:S(2)}, u32[]{:S(2)}) collective-permute-start(bf16[12,128,128]{2,1,0:T(8,128)(2,1)S(1)} %slice.15), channel_id=1, source_target_pairs={{0,8},{8,0},{1,9},{9,1},{2,10},{10,2},{3,11},{11,3},{4,12},{12,4},... | collective-permute-start | bytes 1179656 | tf_op jit(solution)/shard_map/ppermute | solution.py:247
  37.6 0.9 collective-permute-start.3
  38.4 0.0 copy-done
  38.5 10.3 %shard_map.47 = (f32[2048,256]{1,0:T(8,128)S(1)}, f32[2048,128]{1,0:T(8,128)S(1)}, f32[8,128]{1,0:T(8,128)S(1)}, f32[2,5,4,256]{3,2,1,0:T(4,128)S(1)}) custom-call(bf16[32,192,128]{2,1,0:T(8,128)(2,1)S(1)} %all_to_all.10.refs_0_.refs_1_, bf16[32,192,128]{2,1,0:T(8,128)(2,1)S(1)} %all_to_all.10.refs_0_.refs_1_, s32[4,8]{1,0:T(4,128)S(1)} %copy-done), custom_call_target="tpu_custom_call" | custom-call | flops 4294967296 | bytes 6291456 | tf_op jit(solution)/shard_map/pallas_call | solution.py:215
  48.8 0.0 collective-permute-done.refs_1_
  48.8 9.9 %shard_map.48 = (f32[2048,256]{1,0:T(8,128)S(1)}, f32[2048,128]{1,0:T(8,128)S(1)}, f32[8,128]{1,0:T(8,128)S(1)}) custom-call(bf16[32,192,128]{2,1,0:T(8,128)(2,1)S(1)} %all_to_all.10.refs_0_.refs_1_, bf16[32,128,128]{2,1,0:T(8,128)(2,1)S(1)} %collective-permute-done.refs_1_, f32[2048,256]{1,0:T(8,128)S(1)} %get-tuple-element.29.refs_2_, ...), custom_call_target="tpu_custom_call" | custom-call | flops 4294967296 | bytes 6291456 | tf_op jit(solution)/shard_map/pallas_call | solution.py:215
  58.7 0.0 collective-permute-done.1.refs_1_
  58.7 0.1 collective-permute-start.2
  58.8 5.3 %shard_map.49 = (f32[2048,256]{1,0:T(8,128)S(1)}, f32[2048,128]{1,0:T(8,128)S(1)}, f32[8,128]{1,0:T(8,128)S(1)}) custom-call(bf16[32,192,128]{2,1,0:T(8,128)(2,1)S(1)} %all_to_all.10.refs_0_.refs_1_, bf16[12,128,128]{2,1,0:T(8,128)(2,1)S(1)} %collective-permute-done.1.refs_1_, f32[2048,256]{1,0:T(8,128)S(1)} %get-tuple-element.37.refs_2_, ...), custom_call_target="tpu_custom_call" | custom-call | flops 1610612736 | bytes 6291456 | tf_op jit(solution)/shard_map/pallas_call | solution.py:215
  64.2 0.0 collective-permute-done.2.refs_1_
  64.2 5.4 %shard_map.50 = (f32[2048,256]{1,0:T(8,128)S(1)}, f32[2048,128]{1,0:T(8,128)S(1)}, f32[8,128]{1,0:T(8,128)S(1)}) custom-call(bf16[32,192,128]{2,1,0:T(8,128)(2,1)S(1)} %all_to_all.10.refs_0_.refs_1_, bf16[12,128,128]{2,1,0:T(8,128)(2,1)S(1)} %collective-permute-done.2.refs_1_, f32[2048,256]{1,0:T(8,128)S(1)} %get-tuple-element.40.refs_2_, ...), custom_call_target="tpu_custom_call" | custom-call | flops 1610612736 | bytes 6291456 | tf_op jit(solution)/shard_map/pallas_call | solution.py:215
  69.5 0.0 collective-permute-done.3.refs_1_
  69.5 0.6 collective-permute-start.4
  70.1 7.3 %shard_map.51 = (f32[2048,256]{1,0:T(8,128)S(1)}, f32[2048,128]{1,0:T(8,128)S(1)}, f32[8,128]{1,0:T(8,128)S(1)}) custom-call(bf16[32,192,128]{2,1,0:T(8,128)(2,1)S(1)} %all_to_all.10.refs_0_.refs_1_, bf16[20,128,128]{2,1,0:T(8,128)(2,1)S(1)} %collective-permute-done.3.refs_1_, f32[2048,256]{1,0:T(8,128)S(1)} %get-tuple-element.47.refs_2_, ...), custom_call_target="tpu_custom_call" | custom-call | flops 2684354560 | bytes 6291456 | tf_op jit(solution)/shard_map/pallas_call | solution.py:215
  77.4 0.0 collective-permute-done.4.refs_1_
  77.4 7.1 %shard_map.52 = bf16[32,64,128]{2,1,0:T(8,128)(2,1)S(1)} custom-call(bf16[32,192,128]{2,1,0:T(8,128)(2,1)S(1)} %all_to_all.10.refs_0_.refs_1_, bf16[20,128,128]{2,1,0:T(8,128)(2,1)S(1)} %collective-permute-done.4.refs_1_, f32[2048,256]{1,0:T(8,128)S(1)} %get-tuple-element.50.refs_2_, f32[2048,128]{1,0:T(8,128)S(1)} %get-tuple-element.51.refs_3_, ...), custom_call_target="tpu_custom_call" | custom-call | flops 2684354560 | bytes 6291456 | tf_op jit(solution)/shard_map/pallas_call | solution.py:215
  84.5 15.4 %all_to_all.11.in_ref = bf16[32,64,128]{2,1,0:T(8,128)(2,1)S(1)} all-to-all(bf16[32,64,128]{2,1,0:T(8,128)(2,1)S(1)} %shard_map.52), channel_id=1, replica_groups=mesh['xl'=2,'z1'=2,'z0'=2,'xh'=2,'y'=4,'c'=2] {'xl','z1','z0','y'}, dimensions={0} | all-to-all | bytes 1048576 | tf_op jit(solution)/shard_map/all_to_all | solution.py:268
  99.9 0.9 shard_map.53
  (2 shorter events, 0.1 us)
Async XLA Ops:
  34.5 3.9 %copy-start = (s32[4,8]{1,0:T(4,128)S(1)}, s32[4,8]{1,0:T(4,128)}, u32[]{:S(2)}) copy-start(s32[4,8]{1,0:T(4,128)} %refs_2_.1) | copy-start | bytes 388
  34.6 14.2 %collective-permute-start = (bf16[32,128,128]{2,1,0:T(8,128)(2,1)S(1)}, bf16[32,128,128]{2,1,0:T(8,128)(2,1)S(1)}, u32[]{:S(2)}, u32[]{:S(2)}) collective-permute-start(bf16[32,128,128]{2,1,0:T(8,128)(2,1)S(1)} %slice.14), channel_id=1, source_target_pairs={{0,1},{1,0},{2,3},{3,2},{4,5},{5,4},{6,7},{7,6},{8,9},{9,8},{10,11... | collective-permute-start | bytes 3145736 | tf_op jit(solution)/shard_map/ppermute | solution.py:248
  34.7 24.0 %collective-permute-start.1 = (bf16[12,128,128]{2,1,0:T(8,128)(2,1)S(1)}, bf16[12,128,128]{2,1,0:T(8,128)(2,1)S(1)}, u32[]{:S(2)}, u32[]{:S(2)}) collective-permute-start(bf16[12,128,128]{2,1,0:T(8,128)(2,1)S(1)} %slice.15), channel_id=1, source_target_pairs={{0,8},{8,0},{1,9},{9,1},{2,10},{10,2},{3,11},{11,3},{4,12},{12,4},... | collective-permute-start | bytes 1179656 | tf_op jit(solution)/shard_map/ppermute | solution.py:247
  37.6 32.0 %collective-permute-start.3 = (bf16[20,128,128]{2,1,0:T(8,128)(2,1)S(1)}, bf16[20,128,128]{2,1,0:T(8,128)(2,1)S(1)}, u32[]{:S(2)}, u32[]{:S(2)}) collective-permute-start(bf16[20,128,128]{2,1,0:T(8,128)(2,1)S(1)} %slice.16), channel_id=1, source_target_pairs={{0,8},{8,0},{1,9},{9,1},{2,10},{10,2},{3,11},{11,3},{4,12},{12,4},... | collective-permute-start | bytes 1966088 | tf_op jit(solution)/shard_map/ppermute | solution.py:247
  58.7 5.4 %collective-permute-start.2 = (bf16[12,128,128]{2,1,0:T(8,128)(2,1)S(1)}, bf16[12,128,128]{2,1,0:T(8,128)(2,1)S(1)}, u32[]{:S(2)}, u32[]{:S(2)}) collective-permute-start(bf16[12,128,128]{2,1,0:T(8,128)(2,1)S(1)} %collective-permute-done.1.refs_1_), channel_id=1, source_target_pairs={{0,1},{1,0},{2,3},{3,2},{4,5},{5,4},{6,7},{7,6},{8,9},{9,8},{10,11... | collective-permute-start | bytes 1179656 | tf_op jit(solution)/shard_map/ppermute | solution.py:261
  69.5 7.9 %collective-permute-start.4 = (bf16[20,128,128]{2,1,0:T(8,128)(2,1)S(1)}, bf16[20,128,128]{2,1,0:T(8,128)(2,1)S(1)}, u32[]{:S(2)}, u32[]{:S(2)}) collective-permute-start(bf16[20,128,128]{2,1,0:T(8,128)(2,1)S(1)} %collective-permute-done.3.refs_1_), channel_id=1, source_target_pairs={{0,1},{1,0},{2,3},{3,2},{4,5},{5,4},{6,7},{7,6},{8,9},{9,8},{10,11... | collective-permute-start | bytes 1966088 | tf_op jit(solution)/shard_map/ppermute | solution.py:265

commit v4 on v3

--- a/solution.py
+++ b/solution.py
@@ -25,7 +25,7 @@
 PARTS = 2
 STRIP = BAND // PARTS
 CUT = 3
-GROUP = ("xl", "z1", "z0", "y")
+GROUP = ("z1", "z0", "xl", "y")
 SWAP = [(0, 1), (1, 0)]
 NT = (((1,), (1,)), ((), ()))
 VMEM = pl.BlockSpec(memory_space=pltpu.VMEM)
@@ -130,7 +130,7 @@
         scores = lax.dot_general(queries, keys, NT, preferred_element_type=jnp.float32) * SCALE
         bands = []
         for own in range(2):
-            rows = jnp.concatenate([bias[far, pattern(2 * step + own, frame + other)] for other in range(width)], axis=1)
+            rows = jnp.concatenate([bias[far, pattern(own * NEAR + step, (frame + other) % 2 * NEAR + (frame + other) // 2)] for other in range(width)], axis=1)
             bands.append(jnp.broadcast_to(rows[:, None, :], (NEAR, BAND, width * SPAN)).reshape(SPAN, width * SPAN))
         return scores + jnp.concatenate(bands, axis=0)
 

time: 101 us -> 101 us (level)
  no operation moved by 1% of the time
where the time goes in v4:
time: 101 us
  Pallas kernels  48.5 us (48%)
  blocking collectives  47.9 us (47%)
  starting transfers between devices  4.44 us (4%)
    pallas_call x6, Pallas kernels, attend(): pl.pallas_call(functools.partial(attend_kernel, parts, first, last), out_...  45.3 us
    all_to_all x1, blocking collectives, on_device(): lax.all_to_all(parcels, GROUP, split_axis=0, concat_axis=0, tiled=True)  32.1 us
    all_to_all x1, blocking collectives, on_device(): lax.all_to_all(result, GROUP, split_axis=0, concat_axis=0, tiled=True)  15.7 us
    ppermute x2, starting transfers between devices, on_device(): lax.ppermute(part, 'xh', SWAP)  3.69 us
    pallas_call x1, Pallas kernels, on_device(): pl.pallas_call(pack_kernel, out_shape=jax.ShapeDtypeStruct((HEADS, 3 * BA...  2.25 us
  transfers between devices with their start and end apart: 5, of which 0 were waited for; matrix products, arithmetic and copies ran while one was open for 0% of the time, Pallas kernels for 38%

profile of v4, /device:TPU:0, one launch (start us, length us, event | category | flops | bytes accessed | tf_op | source)
XLA Modules:
  0.0 101.1 jit_solution(16320979755961518082)
XLA Ops:
  0.0 2.2 %shard_map.46 = bf16[32,192,128]{2,1,0:T(8,128)(2,1)} custom-call(bf16[1,64,4096]{2,1,0:T(8,128)(2,1)} %q_ref.1, bf16[1,64,4096]{2,1,0:T(8,128)(2,1)} %k_ref.1, bf16[1,64,4096]{2,1,0:T(8,128)(2,1)} %v_ref.1), custom_call_target="tpu_custom_call" | custom-call | bytes 4194304 | tf_op jit(solution)/shard_map/pallas_call | solution.py:231
  2.3 32.1 %all_to_all.10.refs_0_.refs_1_ = bf16[32,192,128]{2,1,0:T(8,128)(2,1)S(1)} all-to-all(bf16[32,192,128]{2,1,0:T(8,128)(2,1)} %shard_map.46), channel_id=1, replica_groups=mesh['xl'=2,'z1'=2,'z0'=2,'xh'=2,'y'=4,'c'=2] {'z1','z0','xl','y'}, dimensions={0} | all-to-all | bytes 3145728 | tf_op jit(solution)/shard_map/all_to_all | solution.py:245
  34.4 0.0 copy-start
  34.4 0.1 slice.14
  34.5 0.1 collective-permute-start
  34.6 2.8 %collective-permute-start.1 = (bf16[12,128,128]{2,1,0:T(8,128)(2,1)S(1)}, bf16[12,128,128]{2,1,0:T(8,128)(2,1)S(1)}, u32[]{:S(2)}, u32[]{:S(2)}) collective-permute-start(bf16[12,128,128]{2,1,0:T(8,128)(2,1)S(1)} %slice.15), channel_id=1, source_target_pairs={{0,8},{8,0},{1,9},{9,1},{2,10},{10,2},{3,11},{11,3},{4,12},{12,4},... | collective-permute-start | bytes 1179656 | tf_op jit(solution)/shard_map/ppermute | solution.py:247
  37.4 0.9 collective-permute-start.3
  38.3 0.0 copy-done
  38.3 10.3 %shard_map.47 = (f32[2048,256]{1,0:T(8,128)S(1)}, f32[2048,128]{1,0:T(8,128)S(1)}, f32[8,128]{1,0:T(8,128)S(1)}, f32[2,5,4,256]{3,2,1,0:T(4,128)S(1)}) custom-call(bf16[32,192,128]{2,1,0:T(8,128)(2,1)S(1)} %all_to_all.10.refs_0_.refs_1_, bf16[32,192,128]{2,1,0:T(8,128)(2,1)S(1)} %all_to_all.10.refs_0_.refs_1_, s32[4,8]{1,0:T(4,128)S(1)} %copy-done), custom_call_target="tpu_custom_call" | custom-call | flops 4294967296 | bytes 6291456 | tf_op jit(solution)/shard_map/pallas_call | solution.py:215
  48.7 0.0 collective-permute-done.refs_1_
  48.7 9.9 %shard_map.48 = (f32[2048,256]{1,0:T(8,128)S(1)}, f32[2048,128]{1,0:T(8,128)S(1)}, f32[8,128]{1,0:T(8,128)S(1)}) custom-call(bf16[32,192,128]{2,1,0:T(8,128)(2,1)S(1)} %all_to_all.10.refs_0_.refs_1_, bf16[32,128,128]{2,1,0:T(8,128)(2,1)S(1)} %collective-permute-done.refs_1_, f32[2048,256]{1,0:T(8,128)S(1)} %get-tuple-element.29.refs_2_, ...), custom_call_target="tpu_custom_call" | custom-call | flops 4294967296 | bytes 6291456 | tf_op jit(solution)/shard_map/pallas_call | solution.py:215
  58.6 0.0 collective-permute-done.1.refs_1_
  58.6 0.1 collective-permute-start.2
  58.7 5.3 %shard_map.49 = (f32[2048,256]{1,0:T(8,128)S(1)}, f32[2048,128]{1,0:T(8,128)S(1)}, f32[8,128]{1,0:T(8,128)S(1)}) custom-call(bf16[32,192,128]{2,1,0:T(8,128)(2,1)S(1)} %all_to_all.10.refs_0_.refs_1_, bf16[12,128,128]{2,1,0:T(8,128)(2,1)S(1)} %collective-permute-done.1.refs_1_, f32[2048,256]{1,0:T(8,128)S(1)} %get-tuple-element.37.refs_2_, ...), custom_call_target="tpu_custom_call" | custom-call | flops 1610612736 | bytes 6291456 | tf_op jit(solution)/shard_map/pallas_call | solution.py:215
  64.1 0.0 collective-permute-done.2.refs_1_
  64.1 5.4 %shard_map.50 = (f32[2048,256]{1,0:T(8,128)S(1)}, f32[2048,128]{1,0:T(8,128)S(1)}, f32[8,128]{1,0:T(8,128)S(1)}) custom-call(bf16[32,192,128]{2,1,0:T(8,128)(2,1)S(1)} %all_to_all.10.refs_0_.refs_1_, bf16[12,128,128]{2,1,0:T(8,128)(2,1)S(1)} %collective-permute-done.2.refs_1_, f32[2048,256]{1,0:T(8,128)S(1)} %get-tuple-element.40.refs_2_, ...), custom_call_target="tpu_custom_call" | custom-call | flops 1610612736 | bytes 6291456 | tf_op jit(solution)/shard_map/pallas_call | solution.py:215
  69.5 0.0 collective-permute-done.3.refs_1_
  69.5 0.6 collective-permute-start.4
  70.1 7.3 %shard_map.51 = (f32[2048,256]{1,0:T(8,128)S(1)}, f32[2048,128]{1,0:T(8,128)S(1)}, f32[8,128]{1,0:T(8,128)S(1)}) custom-call(bf16[32,192,128]{2,1,0:T(8,128)(2,1)S(1)} %all_to_all.10.refs_0_.refs_1_, bf16[20,128,128]{2,1,0:T(8,128)(2,1)S(1)} %collective-permute-done.3.refs_1_, f32[2048,256]{1,0:T(8,128)S(1)} %get-tuple-element.47.refs_2_, ...), custom_call_target="tpu_custom_call" | custom-call | flops 2684354560 | bytes 6291456 | tf_op jit(solution)/shard_map/pallas_call | solution.py:215
  77.4 0.0 collective-permute-done.4.refs_1_
  77.4 7.1 %shard_map.52 = bf16[32,64,128]{2,1,0:T(8,128)(2,1)S(1)} custom-call(bf16[32,192,128]{2,1,0:T(8,128)(2,1)S(1)} %all_to_all.10.refs_0_.refs_1_, bf16[20,128,128]{2,1,0:T(8,128)(2,1)S(1)} %collective-permute-done.4.refs_1_, f32[2048,256]{1,0:T(8,128)S(1)} %get-tuple-element.50.refs_2_, f32[2048,128]{1,0:T(8,128)S(1)} %get-tuple-element.51.refs_3_, ...), custom_call_target="tpu_custom_call" | custom-call | flops 2684354560 | bytes 6291456 | tf_op jit(solution)/shard_map/pallas_call | solution.py:215
  84.4 15.7 %all_to_all.11.in_ref = bf16[32,64,128]{2,1,0:T(8,128)(2,1)S(1)} all-to-all(bf16[32,64,128]{2,1,0:T(8,128)(2,1)S(1)} %shard_map.52), channel_id=1, replica_groups=mesh['xl'=2,'z1'=2,'z0'=2,'xh'=2,'y'=4,'c'=2] {'z1','z0','xl','y'}, dimensions={0} | all-to-all | bytes 1048576 | tf_op jit(solution)/shard_map/all_to_all | solution.py:268
  100.2 0.9 shard_map.53
  (2 shorter events, 0.1 us)
Async XLA Ops:
  34.4 3.9 %copy-start = (s32[4,8]{1,0:T(4,128)S(1)}, s32[4,8]{1,0:T(4,128)}, u32[]{:S(2)}) copy-start(s32[4,8]{1,0:T(4,128)} %refs_2_.1) | copy-start | bytes 388
  34.5 14.2 %collective-permute-start = (bf16[32,128,128]{2,1,0:T(8,128)(2,1)S(1)}, bf16[32,128,128]{2,1,0:T(8,128)(2,1)S(1)}, u32[]{:S(2)}, u32[]{:S(2)}) collective-permute-start(bf16[32,128,128]{2,1,0:T(8,128)(2,1)S(1)} %slice.14), channel_id=1, source_target_pairs={{0,1},{1,0},{2,3},{3,2},{4,5},{5,4},{6,7},{7,6},{8,9},{9,8},{10,11... | collective-permute-start | bytes 3145736 | tf_op jit(solution)/shard_map/ppermute | solution.py:248
  34.6 24.1 %collective-permute-start.1 = (bf16[12,128,128]{2,1,0:T(8,128)(2,1)S(1)}, bf16[12,128,128]{2,1,0:T(8,128)(2,1)S(1)}, u32[]{:S(2)}, u32[]{:S(2)}) collective-permute-start(bf16[12,128,128]{2,1,0:T(8,128)(2,1)S(1)} %slice.15), channel_id=1, source_target_pairs={{0,8},{8,0},{1,9},{9,1},{2,10},{10,2},{3,11},{11,3},{4,12},{12,4},... | collective-permute-start | bytes 1179656 | tf_op jit(solution)/shard_map/ppermute | solution.py:247
  37.4 32.0 %collective-permute-start.3 = (bf16[20,128,128]{2,1,0:T(8,128)(2,1)S(1)}, bf16[20,128,128]{2,1,0:T(8,128)(2,1)S(1)}, u32[]{:S(2)}, u32[]{:S(2)}) collective-permute-start(bf16[20,128,128]{2,1,0:T(8,128)(2,1)S(1)} %slice.16), channel_id=1, source_target_pairs={{0,8},{8,0},{1,9},{9,1},{2,10},{10,2},{3,11},{11,3},{4,12},{12,4},... | collective-permute-start | bytes 1966088 | tf_op jit(solution)/shard_map/ppermute | solution.py:247
  58.6 5.4 %collective-permute-start.2 = (bf16[12,128,128]{2,1,0:T(8,128)(2,1)S(1)}, bf16[12,128,128]{2,1,0:T(8,128)(2,1)S(1)}, u32[]{:S(2)}, u32[]{:S(2)}) collective-permute-start(bf16[12,128,128]{2,1,0:T(8,128)(2,1)S(1)} %collective-permute-done.1.refs_1_), channel_id=1, source_target_pairs={{0,1},{1,0},{2,3},{3,2},{4,5},{5,4},{6,7},{7,6},{8,9},{9,8},{10,11... | collective-permute-start | bytes 1179656 | tf_op jit(solution)/shard_map/ppermute | solution.py:261
  69.5 7.9 %collective-permute-start.4 = (bf16[20,128,128]{2,1,0:T(8,128)(2,1)S(1)}, bf16[20,128,128]{2,1,0:T(8,128)(2,1)S(1)}, u32[]{:S(2)}, u32[]{:S(2)}) collective-permute-start(bf16[20,128,128]{2,1,0:T(8,128)(2,1)S(1)} %collective-permute-done.3.refs_1_), channel_id=1, source_target_pairs={{0,1},{1,0},{2,3},{3,2},{4,5},{5,4},{6,7},{7,6},{8,9},{9,8},{10,11... | collective-permute-start | bytes 1966088 | tf_op jit(solution)/shard_map/ppermute | solution.py:265

commit v5 on v3

--- a/solution.py
+++ b/solution.py
@@ -114,8 +114,11 @@
     tiles = []
     for (base, far, frame), kv_ref in zip(parts, kv_refs):
         count = kv_ref.shape[0] // NEAR
-        for slot in range(0, count, 2):
-            tiles.append((kv_ref, base, far, slot, min(2, count - slot), frame + slot))
+        slot = 0
+        while slot < count:
+            width = 3 if (count - slot) % 2 else 2
+            tiles.append((kv_ref, base, far, slot, width, frame + slot))
+            slot += width
 
     def cut(tile, first):
         kv_ref, _, _, slot, width, _ = tile

time: 101 us -> 101 us (level)
  transfers between devices with their start and end apart: 5 -> 5, of which waited for: 0 -> 0; matrix products, arithmetic and copies ran while one was open for 0% -> 0% of each run, Pallas kernels for 38% -> 37%
where the time goes in v5:
time: 101 us
  Pallas kernels  48.5 us (48%)
  blocking collectives  47.6 us (47%)
  starting transfers between devices  4.43 us (4%)
    pallas_call x6, Pallas kernels, attend(): pl.pallas_call(functools.partial(attend_kernel, parts, first, last), out_...  45.4 us
    all_to_all x1, blocking collectives, on_device(): lax.all_to_all(parcels, GROUP, split_axis=0, concat_axis=0, tiled=True)  32.2 us
    all_to_all x1, blocking collectives, on_device(): lax.all_to_all(result, GROUP, split_axis=0, concat_axis=0, tiled=True)  15.4 us
    ppermute x2, starting transfers between devices, on_device(): lax.ppermute(part, 'xh', SWAP)  3.69 us
    pallas_call x1, Pallas kernels, on_device(): pl.pallas_call(pack_kernel, out_shape=jax.ShapeDtypeStruct((HEADS, 3 * BA...  2.25 us
  transfers between devices with their start and end apart: 5, of which 0 were waited for; matrix products, arithmetic and copies ran while one was open for 0% of the time, Pallas kernels for 37%

profile of v5, /device:TPU:0, one launch (start us, length us, event | category | flops | bytes accessed | tf_op | source)
XLA Modules:
  0.0 100.9 jit_solution(10576246683374927117)
XLA Ops:
  0.0 2.2 %shard_map.46 = bf16[32,192,128]{2,1,0:T(8,128)(2,1)} custom-call(bf16[1,64,4096]{2,1,0:T(8,128)(2,1)} %q_ref.1, bf16[1,64,4096]{2,1,0:T(8,128)(2,1)} %k_ref.1, bf16[1,64,4096]{2,1,0:T(8,128)(2,1)} %v_ref.1), custom_call_target="tpu_custom_call" | custom-call | bytes 4194304 | tf_op jit(solution)/shard_map/pallas_call | solution.py:234
  2.3 32.2 %all_to_all.10.refs_0_.refs_1_ = bf16[32,192,128]{2,1,0:T(8,128)(2,1)S(1)} all-to-all(bf16[32,192,128]{2,1,0:T(8,128)(2,1)} %shard_map.46), channel_id=1, replica_groups=mesh['xl'=2,'z1'=2,'z0'=2,'xh'=2,'y'=4,'c'=2] {'xl','z1','z0','y'}, dimensions={0} | all-to-all | bytes 3145728 | tf_op jit(solution)/shard_map/all_to_all | solution.py:248
  34.5 0.0 copy-start
  34.5 0.1 slice.14
  34.6 0.1 collective-permute-start
  34.7 2.8 %collective-permute-start.1 = (bf16[12,128,128]{2,1,0:T(8,128)(2,1)S(1)}, bf16[12,128,128]{2,1,0:T(8,128)(2,1)S(1)}, u32[]{:S(2)}, u32[]{:S(2)}) collective-permute-start(bf16[12,128,128]{2,1,0:T(8,128)(2,1)S(1)} %slice.15), channel_id=1, source_target_pairs={{0,8},{8,0},{1,9},{9,1},{2,10},{10,2},{3,11},{11,3},{4,12},{12,4},... | collective-permute-start | bytes 1179656 | tf_op jit(solution)/shard_map/ppermute | solution.py:250
  37.6 0.9 collective-permute-start.3
  38.4 0.0 copy-done
  38.5 10.3 %shard_map.47 = (f32[2048,256]{1,0:T(8,128)S(1)}, f32[2048,128]{1,0:T(8,128)S(1)}, f32[8,128]{1,0:T(8,128)S(1)}, f32[2,5,4,256]{3,2,1,0:T(4,128)S(1)}) custom-call(bf16[32,192,128]{2,1,0:T(8,128)(2,1)S(1)} %all_to_all.10.refs_0_.refs_1_, bf16[32,192,128]{2,1,0:T(8,128)(2,1)S(1)} %all_to_all.10.refs_0_.refs_1_, s32[4,8]{1,0:T(4,128)S(1)} %copy-done), custom_call_target="tpu_custom_call" | custom-call | flops 4294967296 | bytes 6291456 | tf_op jit(solution)/shard_map/pallas_call | solution.py:218
  48.8 0.0 collective-permute-done.refs_1_
  48.8 9.9 %shard_map.48 = (f32[2048,256]{1,0:T(8,128)S(1)}, f32[2048,128]{1,0:T(8,128)S(1)}, f32[8,128]{1,0:T(8,128)S(1)}) custom-call(bf16[32,192,128]{2,1,0:T(8,128)(2,1)S(1)} %all_to_all.10.refs_0_.refs_1_, bf16[32,128,128]{2,1,0:T(8,128)(2,1)S(1)} %collective-permute-done.refs_1_, f32[2048,256]{1,0:T(8,128)S(1)} %get-tuple-element.29.refs_2_, ...), custom_call_target="tpu_custom_call" | custom-call | flops 4294967296 | bytes 6291456 | tf_op jit(solution)/shard_map/pallas_call | solution.py:218
  58.7 0.0 collective-permute-done.1.refs_1_
  58.7 0.1 collective-permute-start.2
  58.8 4.8 %shard_map.49 = (f32[2048,256]{1,0:T(8,128)S(1)}, f32[2048,128]{1,0:T(8,128)S(1)}, f32[8,128]{1,0:T(8,128)S(1)}) custom-call(bf16[32,192,128]{2,1,0:T(8,128)(2,1)S(1)} %all_to_all.10.refs_0_.refs_1_, bf16[12,128,128]{2,1,0:T(8,128)(2,1)S(1)} %collective-permute-done.1.refs_1_, f32[2048,256]{1,0:T(8,128)S(1)} %get-tuple-element.37.refs_2_, ...), custom_call_target="tpu_custom_call" | custom-call | flops 1610612736 | bytes 6291456 | tf_op jit(solution)/shard_map/pallas_call | solution.py:218
  63.6 0.0 collective-permute-done.2.refs_1_
  63.6 4.8 %shard_map.50 = (f32[2048,256]{1,0:T(8,128)S(1)}, f32[2048,128]{1,0:T(8,128)S(1)}, f32[8,128]{1,0:T(8,128)S(1)}) custom-call(bf16[32,192,128]{2,1,0:T(8,128)(2,1)S(1)} %all_to_all.10.refs_0_.refs_1_, bf16[12,128,128]{2,1,0:T(8,128)(2,1)S(1)} %collective-permute-done.2.refs_1_, f32[2048,256]{1,0:T(8,128)S(1)} %get-tuple-element.40.refs_2_, ...), custom_call_target="tpu_custom_call" | custom-call | flops 1610612736 | bytes 6291456 | tf_op jit(solution)/shard_map/pallas_call | solution.py:218
  68.5 0.0 collective-permute-done.3.refs_1_
  68.5 0.6 collective-permute-start.4
  69.1 7.8 %shard_map.51 = (f32[2048,256]{1,0:T(8,128)S(1)}, f32[2048,128]{1,0:T(8,128)S(1)}, f32[8,128]{1,0:T(8,128)S(1)}) custom-call(bf16[32,192,128]{2,1,0:T(8,128)(2,1)S(1)} %all_to_all.10.refs_0_.refs_1_, bf16[20,128,128]{2,1,0:T(8,128)(2,1)S(1)} %collective-permute-done.3.refs_1_, f32[2048,256]{1,0:T(8,128)S(1)} %get-tuple-element.47.refs_2_, ...), custom_call_target="tpu_custom_call" | custom-call | flops 2684354560 | bytes 6291456 | tf_op jit(solution)/shard_map/pallas_call | solution.py:218
  76.9 0.0 collective-permute-done.4.refs_1_
  76.9 7.6 %shard_map.52 = bf16[32,64,128]{2,1,0:T(8,128)(2,1)S(1)} custom-call(bf16[32,192,128]{2,1,0:T(8,128)(2,1)S(1)} %all_to_all.10.refs_0_.refs_1_, bf16[20,128,128]{2,1,0:T(8,128)(2,1)S(1)} %collective-permute-done.4.refs_1_, f32[2048,256]{1,0:T(8,128)S(1)} %get-tuple-element.50.refs_2_, f32[2048,128]{1,0:T(8,128)S(1)} %get-tuple-element.51.refs_3_, ...), custom_call_target="tpu_custom_call" | custom-call | flops 2684354560 | bytes 6291456 | tf_op jit(solution)/shard_map/pallas_call | solution.py:218
  84.6 15.4 %all_to_all.11.in_ref = bf16[32,64,128]{2,1,0:T(8,128)(2,1)S(1)} all-to-all(bf16[32,64,128]{2,1,0:T(8,128)(2,1)S(1)} %shard_map.52), channel_id=1, replica_groups=mesh['xl'=2,'z1'=2,'z0'=2,'xh'=2,'y'=4,'c'=2] {'xl','z1','z0','y'}, dimensions={0} | all-to-all | bytes 1048576 | tf_op jit(solution)/shard_map/all_to_all | solution.py:271
  100.0 0.9 shard_map.53
  (2 shorter events, 0.1 us)
Async XLA Ops:
  34.5 3.9 %copy-start = (s32[4,8]{1,0:T(4,128)S(1)}, s32[4,8]{1,0:T(4,128)}, u32[]{:S(2)}) copy-start(s32[4,8]{1,0:T(4,128)} %refs_2_.1) | copy-start | bytes 388
  34.6 14.2 %collective-permute-start = (bf16[32,128,128]{2,1,0:T(8,128)(2,1)S(1)}, bf16[32,128,128]{2,1,0:T(8,128)(2,1)S(1)}, u32[]{:S(2)}, u32[]{:S(2)}) collective-permute-start(bf16[32,128,128]{2,1,0:T(8,128)(2,1)S(1)} %slice.14), channel_id=1, source_target_pairs={{0,1},{1,0},{2,3},{3,2},{4,5},{5,4},{6,7},{7,6},{8,9},{9,8},{10,11... | collective-permute-start | bytes 3145736 | tf_op jit(solution)/shard_map/ppermute | solution.py:251
  34.7 24.0 %collective-permute-start.1 = (bf16[12,128,128]{2,1,0:T(8,128)(2,1)S(1)}, bf16[12,128,128]{2,1,0:T(8,128)(2,1)S(1)}, u32[]{:S(2)}, u32[]{:S(2)}) collective-permute-start(bf16[12,128,128]{2,1,0:T(8,128)(2,1)S(1)} %slice.15), channel_id=1, source_target_pairs={{0,8},{8,0},{1,9},{9,1},{2,10},{10,2},{3,11},{11,3},{4,12},{12,4},... | collective-permute-start | bytes 1179656 | tf_op jit(solution)/shard_map/ppermute | solution.py:250
  37.6 30.9 %collective-permute-start.3 = (bf16[20,128,128]{2,1,0:T(8,128)(2,1)S(1)}, bf16[20,128,128]{2,1,0:T(8,128)(2,1)S(1)}, u32[]{:S(2)}, u32[]{:S(2)}) collective-permute-start(bf16[20,128,128]{2,1,0:T(8,128)(2,1)S(1)} %slice.16), channel_id=1, source_target_pairs={{0,8},{8,0},{1,9},{9,1},{2,10},{10,2},{3,11},{11,3},{4,12},{12,4},... | collective-permute-start | bytes 1966088 | tf_op jit(solution)/shard_map/ppermute | solution.py:250
  58.7 4.9 %collective-permute-start.2 = (bf16[12,128,128]{2,1,0:T(8,128)(2,1)S(1)}, bf16[12,128,128]{2,1,0:T(8,128)(2,1)S(1)}, u32[]{:S(2)}, u32[]{:S(2)}) collective-permute-start(bf16[12,128,128]{2,1,0:T(8,128)(2,1)S(1)} %collective-permute-done.1.refs_1_), channel_id=1, source_target_pairs={{0,1},{1,0},{2,3},{3,2},{4,5},{5,4},{6,7},{7,6},{8,9},{9,8},{10,11... | collective-permute-start | bytes 1179656 | tf_op jit(solution)/shard_map/ppermute | solution.py:264
  68.5 8.4 %collective-permute-start.4 = (bf16[20,128,128]{2,1,0:T(8,128)(2,1)S(1)}, bf16[20,128,128]{2,1,0:T(8,128)(2,1)S(1)}, u32[]{:S(2)}, u32[]{:S(2)}) collective-permute-start(bf16[20,128,128]{2,1,0:T(8,128)(2,1)S(1)} %collective-permute-done.3.refs_1_), channel_id=1, source_target_pairs={{0,1},{1,0},{2,3},{3,2},{4,5},{5,4},{6,7},{7,6},{8,9},{9,8},{10,11... | collective-permute-start | bytes 1966088 | tf_op jit(solution)/shard_map/ppermute | solution.py:268
